TPU v7x, 32 devices: a whole 2x2x4 slice. The times are simulated.
32 devices in a mesh: gx: 16 (over z, y, core), gy: 2 (over x).
Axes of the slice: x: 2, y: 2, z: 4, core: 2. Of those that a mesh axis runs over, the one named last changes fastest.
Arguments:
- rhs: float32 [8, 32, 16, 128], P(None, 'gx', 'gy'), may hold values from -6 to 6
- classes: int32 [32, 16, 128], P('gx', 'gy'), may hold values from 0 to 3
- supports: int32 [32, 16, 128], P('gx', 'gy'), may hold values 0 or 1
Outputs:
- solution: float32 [8, 32, 16, 128], P(None, 'gx', 'gy')
- residual: float32 [8, 32, 16, 128], P(None, 'gx', 'gy')
- new_direction: float32 [8, 32, 16, 128], P(None, 'gx', 'gy')
Inputs may be any that keep to these rules, and one draw needn't show every extreme that they name: `supports`: 1 marks a grounded node.
All inputs are finite; a program needn't handle non-finite values. No bound on the sum of `supports` on one device may be relied on, other than what follows from the above.
Results may differ from a plain program's by a relative error of at most 0.0003.
Values sent between devices are 32-bit elements; how exact they have to be, the bound alone decides.
A program may use at most 64 MiB of HBM per device.

v0:
```python
import jax
import jax.numpy as jnp
from jax import lax
from jax.sharding import PartitionSpec as P

COARSE_SWEEPS = 2


SPRING = 8.0
OMEGA = 0.6
DAMP = 0.5
SELF_WEIGHT = 5.0 / 12.0


def passed_along(shard, axis, by):
    devices = lax.axis_size(axis)
    pairs = [(i, i + by) for i in range(devices) if 0 <= i + by < devices]
    return lax.ppermute(shard, axis, pairs)


def with_halo(shard, sides, width):
    for axis, dim in sides:
        devices, length = (lax.axis_size(axis), shard.shape[dim])
        up = [(i, (i + 1) % devices) for i in range(devices - 1)]
        down = [(j, i) for i, j in up]
        last = lax.slice_in_dim(shard, length - width, length, axis=dim)
        first = lax.slice_in_dim(shard, 0, width, axis=dim)
        before = lax.ppermute(last, axis, up)
        after = lax.ppermute(first, axis, down)
        shard = jnp.concatenate([before, shard, after], axis=dim)
    return shard


def stiffness(classes):
    density = (classes.astype(jnp.float32) + 1.0) / 4.0
    return 0.001 + density * density * density


def hex_product(padded, scale_ext):
    nx = scale_ext.shape[0] - 1
    ny = scale_ext.shape[1] - 1
    nz = scale_ext.shape[2] - 1
    corners = {}
    for a in (0, 1):
        for b in (0, 1):
            for c in (0, 1):
                corners[a, b, c] = padded[..., a : a + nx + 1, b : b + ny + 1, c : c + nz + 1]
    summed = sum(corners.values())
    result = None
    for key in corners:
        a, b, c = key
        corner = corners[key]
        adjacent = corners[1 - a, b, c] + corners[a, 1 - b, c] + corners[a, b, 1 - c]
        weighted = scale_ext * (SELF_WEIGHT * corner + adjacent / 12.0 - summed / 12.0)
        piece = weighted[..., 1 - a : 1 - a + nx, 1 - b : 1 - b + ny, 1 - c : 1 - c + nz]
        result = piece if result is None else result + piece
    return result


def prolong(field):
    k, a, b, c = field.shape
    wide = jnp.broadcast_to(field[:, :, None, :, None, :, None], (k, a, 2, b, 2, c, 2))
    return wide.reshape(k, 2 * a, 2 * b, 2 * c)


def restrict(field):
    k, a, b, c = field.shape
    return field.reshape(k, a // 2, 2, b // 2, 2, c // 2, 2).sum(axis=(2, 4, 6))


def inner_block(left, right):
    count = left.shape[0]
    return jnp.dot(
        left.reshape(count, -1), right.reshape(count, -1).T, precision=lax.Precision.HIGHEST
    )


def recombine(coef, field):
    count = field.shape[0]
    return jnp.dot(coef.T, field.reshape(count, -1), precision=lax.Precision.HIGHEST).reshape(
        field.shape
    )


def spd_solve(matrix, right):
    lower = jnp.linalg.cholesky(matrix)
    middle = lax.linalg.triangular_solve(lower, right, left_side=True, lower=True)
    return lax.linalg.triangular_solve(lower, middle, left_side=True, lower=True, transpose_a=True)


def local(rhs, classes, supports):
    scale = stiffness(classes)
    next_plane_x = passed_along(scale[:1], "gx", -1)
    scale_x = jnp.concatenate([scale, next_plane_x], axis=0)
    next_plane_y = passed_along(scale_x[:, :1], "gy", -1)
    scale_ext = jnp.concatenate([scale_x, next_plane_y], axis=1)
    scale_ext = jnp.pad(scale_ext, ((0, 0), (0, 0), (0, 1)))
    support = supports.astype(jnp.float32)
    nx, ny, nz = support.shape
    diagonal = SPRING * support
    for a in (0, 1):
        for b in (0, 1):
            for c in (0, 1):
                diagonal = diagonal + scale_ext[a : a + nx, b : b + ny, c : c + nz] / 3.0
    coarse_step = DAMP / restrict(diagonal[None])[0]

    def fine_apply(field):
        padded = with_halo(field, (("gx", 1), ("gy", 2)), 1)
        padded = jnp.pad(padded, ((0, 0), (0, 0), (0, 0), (1, 1)))
        return hex_product(padded, scale_ext) + SPRING * support * field

    def coarse_apply(coarse):
        return restrict(fine_apply(prolong(coarse)))

    def precondition(source):
        smoothed = OMEGA * source / diagonal
        coarse_res = restrict(source - fine_apply(smoothed))
        coarse = coarse_step * coarse_res
        for sweep in range(COARSE_SWEEPS):
            coarse = coarse + coarse_step * (coarse_res - coarse_apply(coarse))
        smoothed = smoothed + prolong(coarse)
        return smoothed + OMEGA * (source - fine_apply(smoothed)) / diagonal

    first_prec = precondition(rhs)
    applied = fine_apply(first_prec)
    curvature, projection = lax.psum(
        (inner_block(first_prec, applied), inner_block(first_prec, rhs)), ("gx", "gy")
    )
    curvature = 0.5 * (curvature + curvature.T)
    step_coef = spd_solve(curvature, projection)
    solution = recombine(step_coef, first_prec)
    residual = rhs - recombine(step_coef, applied)
    next_prec = precondition(residual)
    coupling = lax.psum(inner_block(applied, next_prec), ("gx", "gy"))
    turn_coef = -spd_solve(curvature, coupling)
    new_direction = next_prec + recombine(turn_coef, first_prec)
    return (solution, residual, new_direction)


def solution(mesh):
    placed = (P(None, "gx", "gy", None), P("gx", "gy", None), P("gx", "gy", None))
    return jax.shard_map(
        local,
        mesh=mesh,
        in_specs=placed,
        out_specs=(P(None, "gx", "gy", None), P(None, "gx", "gy", None), P(None, "gx", "gy", None)),
        check_vma=False,
    )
```

profile of v0, /device:TPU:0, one launch (start us, length us, event | category | flops | bytes accessed | tf_op | source)
XLA Modules:
  0.0 254.2 jit_solution(15999518978324257855)
XLA Ops:
  5.8 4.5 %collective-permute-done.1 = f32[3,1,128]{2,1,0:T(1,128)S(1)} collective-permute-done((f32[3,1,128]{2,1,0:T(1,128)S(1)}, f32[3,1,128]{2,1,0:T(1,128)S(1)}, u32[]{:S(2)}, u32[]{:S(2)}) %collective-permute-start.1) | collective-permute-done | bytes 1568 | tf_op jit(solution)/shard_map/ppermute | solution.py:18
  11.2 3.7 %collective-permute-start.2 = (f32[8,1,8,128]{3,0,2,1:T(8,128)S(1)}, f32[8,1,8,128]{3,0,2,1:T(8,128)S(1)}, u32[]{:S(2)}, u32[]{:S(2)}) collective-permute-start(f32[8,1,8,128]{3,0,2,1:T(8,128)S(1)} %get-tuple-element.162), channel_id=1, source_target_pairs={{0,2},{2,4},{4,6},{6,8},{8,10},{10,12},{12,14},{14,16},{16,18},{18... | collective-permute-start | bytes 98312 | tf_op jit(solution)/shard_map/ppermute | solution.py:28
  21.7 4.2 %collective-permute-done.5 = f32[8,4,1,128]{3,0,2,1:T(8,128)S(1)} collective-permute-done((f32[8,4,1,128]{3,0,2,1:T(8,128)S(1)}, f32[8,4,1,128]{3,0,2,1:T(8,128)S(1)}, u32[]{:S(2)}, u32[]{:S(2)}) %collective-permute-start.5) | collective-permute-done | bytes 16416 | tf_op jit(solution)/shard_map/ppermute | solution.py:29
  28.1 3.1 %collective-permute-start.6 = (f32[8,1,8,128]{3,0,2,1:T(8,128)S(1)}, f32[8,1,8,128]{3,0,2,1:T(8,128)S(1)}, u32[]{:S(2)}, u32[]{:S(2)}) collective-permute-start(f32[8,1,8,128]{3,0,2,1:T(8,128)S(1)} %copy.53), channel_id=1, source_target_pairs={{0,2},{2,4},{4,6},{6,8},{8,10},{10,12},{12,14},{14,16},{16,18},{18... | collective-permute-start | bytes 98312 | tf_op jit(solution)/shard_map/ppermute | solution.py:28
  38.4 4.2 %collective-permute-done.9 = f32[8,4,1,128]{3,0,2,1:T(8,128)S(1)} collective-permute-done((f32[8,4,1,128]{3,0,2,1:T(8,128)S(1)}, f32[8,4,1,128]{3,0,2,1:T(8,128)S(1)}, u32[]{:S(2)}, u32[]{:S(2)}) %collective-permute-start.9) | collective-permute-done | bytes 16416 | tf_op jit(solution)/shard_map/ppermute | solution.py:29
  44.7 3.6 %collective-permute-start.10 = (f32[8,1,8,128]{3,0,2,1:T(8,128)S(1)}, f32[8,1,8,128]{3,0,2,1:T(8,128)S(1)}, u32[]{:S(2)}, u32[]{:S(2)}) collective-permute-start(f32[8,1,8,128]{3,0,2,1:T(8,128)S(1)} %copy.57), channel_id=1, source_target_pairs={{0,2},{2,4},{4,6},{6,8},{8,10},{10,12},{12,14},{14,16},{16,18},{18... | collective-permute-start | bytes 98312 | tf_op jit(solution)/shard_map/ppermute | solution.py:28
  55.7 4.2 %collective-permute-done.13 = f32[8,4,1,128]{3,0,2,1:T(8,128)S(1)} collective-permute-done((f32[8,4,1,128]{3,0,2,1:T(8,128)S(1)}, f32[8,4,1,128]{3,0,2,1:T(8,128)S(1)}, u32[]{:S(2)}, u32[]{:S(2)}) %collective-permute-start.13) | collective-permute-done | bytes 16416 | tf_op jit(solution)/shard_map/ppermute | solution.py:29
  62.1 3.8 %collective-permute-start.14 = (f32[8,1,8,128]{3,0,2,1:T(8,128)S(1)}, f32[8,1,8,128]{3,0,2,1:T(8,128)S(1)}, u32[]{:S(2)}, u32[]{:S(2)}) collective-permute-start(f32[8,1,8,128]{3,0,2,1:T(8,128)S(1)} %get-tuple-element.160), channel_id=1, source_target_pairs={{0,2},{2,4},{4,6},{6,8},{8,10},{10,12},{12,14},{14,16},{16,18},{18... | collective-permute-start | bytes 98312 | tf_op jit(solution)/shard_map/ppermute | solution.py:28
  67.2 3.0 %collective-permute-done.15 = f32[8,1,8,128]{3,0,2,1:T(8,128)S(1)} collective-permute-done((f32[8,1,8,128]{3,0,2,1:T(8,128)S(1)}, f32[8,1,8,128]{3,0,2,1:T(8,128)S(1)}, u32[]{:S(2)}, u32[]{:S(2)}) %collective-permute-start.15) | collective-permute-done | bytes 32800 | tf_op jit(solution)/shard_map/ppermute | solution.py:29
  73.2 4.2 %collective-permute-done.17 = f32[8,4,1,128]{3,0,2,1:T(8,128)S(1)} collective-permute-done((f32[8,4,1,128]{3,0,2,1:T(8,128)S(1)}, f32[8,4,1,128]{3,0,2,1:T(8,128)S(1)}, u32[]{:S(2)}, u32[]{:S(2)}) %collective-permute-start.17) | collective-permute-done | bytes 16416 | tf_op jit(solution)/shard_map/ppermute | solution.py:29
  78.5 3.8 %collective-permute-start.18 = (f32[8,1,8,128]{3,0,2,1:T(8,128)S(1)}, f32[8,1,8,128]{3,0,2,1:T(8,128)S(1)}, u32[]{:S(2)}, u32[]{:S(2)}) collective-permute-start(f32[8,1,8,128]{3,0,2,1:T(8,128)S(1)} %get-tuple-element.158), channel_id=1, source_target_pairs={{0,2},{2,4},{4,6},{6,8},{8,10},{10,12},{12,14},{14,16},{16,18},{18... | collective-permute-start | bytes 98312 | tf_op jit(solution)/shard_map/ppermute | solution.py:28
  83.6 3.0 %collective-permute-done.19 = f32[8,1,8,128]{3,0,2,1:T(8,128)S(1)} collective-permute-done((f32[8,1,8,128]{3,0,2,1:T(8,128)S(1)}, f32[8,1,8,128]{3,0,2,1:T(8,128)S(1)}, u32[]{:S(2)}, u32[]{:S(2)}) %collective-permute-start.19) | collective-permute-done | bytes 32800 | tf_op jit(solution)/shard_map/ppermute | solution.py:29
  89.7 4.1 %collective-permute-done.21 = f32[8,4,1,128]{3,0,2,1:T(8,128)S(1)} collective-permute-done((f32[8,4,1,128]{3,0,2,1:T(8,128)S(1)}, f32[8,4,1,128]{3,0,2,1:T(8,128)S(1)}, u32[]{:S(2)}, u32[]{:S(2)}) %collective-permute-start.21) | collective-permute-done | bytes 16416 | tf_op jit(solution)/shard_map/ppermute | solution.py:29
  95.1 43.5 %all-reduce.10 = (f32[8,8]{1,0:T(8,128)S(1)}, f32[8,8]{1,0:T(8,128)S(1)}) all-reduce(f32[8,8]{1,0:T(8,128)S(1)} %convolution_bitcast_fusion.2, f32[8,8]{1,0:T(8,128)S(1)} %convolution_bitcast_fusion.3), channel_id=1, replica_groups=mesh['gx'=16,'gy'=2] {'gx','gy'}, use_global_device_ids=true, to_apply=%region_11.13 | all-reduce | flops 128 | bytes 1024 | tf_op jit(solution)/shard_map/psum | solution.py:126
  144.7 4.3 %collective-permute-done.23 = f32[8,1,8,128]{3,0,2,1:T(8,128)S(1)} collective-permute-done((f32[8,1,8,128]{3,0,2,1:T(8,128)S(1)}, f32[8,1,8,128]{3,0,2,1:T(8,128)S(1)}, u32[]{:S(2)}, u32[]{:S(2)}) %collective-permute-start.23) | collective-permute-done | bytes 32800 | tf_op jit(solution)/shard_map/ppermute | solution.py:29
  152.4 4.1 %collective-permute-done.25 = f32[8,4,1,128]{3,0,2,1:T(8,128)S(1)} collective-permute-done((f32[8,4,1,128]{3,0,2,1:T(8,128)S(1)}, f32[8,4,1,128]{3,0,2,1:T(8,128)S(1)}, u32[]{:S(2)}, u32[]{:S(2)}) %collective-permute-start.25) | collective-permute-done | bytes 16416 | tf_op jit(solution)/shard_map/ppermute | solution.py:29
  158.7 3.1 %collective-permute-start.26 = (f32[8,1,8,128]{3,0,2,1:T(8,128)S(1)}, f32[8,1,8,128]{3,0,2,1:T(8,128)S(1)}, u32[]{:S(2)}, u32[]{:S(2)}) collective-permute-start(f32[8,1,8,128]{3,0,2,1:T(8,128)S(1)} %copy.72), channel_id=1, source_target_pairs={{0,2},{2,4},{4,6},{6,8},{8,10},{10,12},{12,14},{14,16},{16,18},{18... | collective-permute-start | bytes 98312 | tf_op jit(solution)/shard_map/ppermute | solution.py:28
  163.3 3.0 %collective-permute-done.27 = f32[8,1,8,128]{3,0,2,1:T(8,128)S(1)} collective-permute-done((f32[8,1,8,128]{3,0,2,1:T(8,128)S(1)}, f32[8,1,8,128]{3,0,2,1:T(8,128)S(1)}, u32[]{:S(2)}, u32[]{:S(2)}) %collective-permute-start.27) | collective-permute-done | bytes 32800 | tf_op jit(solution)/shard_map/ppermute | solution.py:29
  169.3 4.2 %collective-permute-done.29 = f32[8,4,1,128]{3,0,2,1:T(8,128)S(1)} collective-permute-done((f32[8,4,1,128]{3,0,2,1:T(8,128)S(1)}, f32[8,4,1,128]{3,0,2,1:T(8,128)S(1)}, u32[]{:S(2)}, u32[]{:S(2)}) %collective-permute-start.29) | collective-permute-done | bytes 16416 | tf_op jit(solution)/shard_map/ppermute | solution.py:29
  175.7 3.8 %collective-permute-start.30 = (f32[8,1,8,128]{3,0,2,1:T(8,128)S(1)}, f32[8,1,8,128]{3,0,2,1:T(8,128)S(1)}, u32[]{:S(2)}, u32[]{:S(2)}) collective-permute-start(f32[8,1,8,128]{3,0,2,1:T(8,128)S(1)} %copy.76), channel_id=1, source_target_pairs={{0,2},{2,4},{4,6},{6,8},{8,10},{10,12},{12,14},{14,16},{16,18},{18... | collective-permute-start | bytes 98312 | tf_op jit(solution)/shard_map/ppermute | solution.py:28
  186.8 4.2 %collective-permute-done.33 = f32[8,4,1,128]{3,0,2,1:T(8,128)S(1)} collective-permute-done((f32[8,4,1,128]{3,0,2,1:T(8,128)S(1)}, f32[8,4,1,128]{3,0,2,1:T(8,128)S(1)}, u32[]{:S(2)}, u32[]{:S(2)}) %collective-permute-start.33) | collective-permute-done | bytes 16416 | tf_op jit(solution)/shard_map/ppermute | solution.py:29
  193.2 3.8 %collective-permute-start.34 = (f32[8,1,8,128]{3,0,2,1:T(8,128)S(1)}, f32[8,1,8,128]{3,0,2,1:T(8,128)S(1)}, u32[]{:S(2)}, u32[]{:S(2)}) collective-permute-start(f32[8,1,8,128]{3,0,2,1:T(8,128)S(1)} %get-tuple-element.154), channel_id=1, source_target_pairs={{0,2},{2,4},{4,6},{6,8},{8,10},{10,12},{12,14},{14,16},{16,18},{18... | collective-permute-start | bytes 98312 | tf_op jit(solution)/shard_map/ppermute | solution.py:28
  198.3 3.0 %collective-permute-done.35 = f32[8,1,8,128]{3,0,2,1:T(8,128)S(1)} collective-permute-done((f32[8,1,8,128]{3,0,2,1:T(8,128)S(1)}, f32[8,1,8,128]{3,0,2,1:T(8,128)S(1)}, u32[]{:S(2)}, u32[]{:S(2)}) %collective-permute-start.35) | collective-permute-done | bytes 32800 | tf_op jit(solution)/shard_map/ppermute | solution.py:29
  209.9 43.1 %psum.23 = f32[8,8]{1,0:T(8,128)S(1)} all-reduce(f32[8,8]{1,0:T(8,128)S(1)} %convolution_bitcast_fusion), channel_id=1, replica_groups=mesh['gx'=16,'gy'=2] {'gx','gy'}, use_global_device_ids=true, to_apply=%region_18.22 | all-reduce | flops 64 | bytes 512 | tf_op jit(solution)/shard_map/psum | solution.py:134
  (179 shorter events, 83.4 us)
Async XLA Ops:
  4.4 5.9 %collective-permute-start.1 = (f32[3,1,128]{2,1,0:T(1,128)S(1)}, f32[3,1,128]{2,1,0:T(1,128)S(1)}, u32[]{:S(2)}, u32[]{:S(2)}) collective-permute-start(f32[3,1,128]{2,1,0:T(1,128)S(1)} %pad_maximum_fusion.29), channel_id=1, source_target_pairs={{1,0},{3,2},{5,4},{7,6},{9,8},{11,10},{13,12},{15,14},{17,16},{19,... | collective-permute-start | bytes 4616 | tf_op jit(solution)/shard_map/ppermute | solution.py:18
  11.2 5.3 %collective-permute-start.2 = (f32[8,1,8,128]{3,0,2,1:T(8,128)S(1)}, f32[8,1,8,128]{3,0,2,1:T(8,128)S(1)}, u32[]{:S(2)}, u32[]{:S(2)}) collective-permute-start(f32[8,1,8,128]{3,0,2,1:T(8,128)S(1)} %get-tuple-element.162), channel_id=1, source_target_pairs={{0,2},{2,4},{4,6},{6,8},{8,10},{10,12},{12,14},{14,16},{16,18},{18... | collective-permute-start | bytes 98312 | tf_op jit(solution)/shard_map/ppermute | solution.py:28
  20.3 5.6 %collective-permute-start.5 = (f32[8,4,1,128]{3,0,2,1:T(8,128)S(1)}, f32[8,4,1,128]{3,0,2,1:T(8,128)S(1)}, u32[]{:S(2)}, u32[]{:S(2)}) collective-permute-start(f32[8,4,1,128]{3,0,2,1:T(8,128)S(1)} %get-tuple-element.153), channel_id=1, source_target_pairs={{1,0},{3,2},{5,4},{7,6},{9,8},{11,10},{13,12},{15,14},{17,16},{19,... | collective-permute-start | bytes 49160 | tf_op jit(solution)/shard_map/ppermute | solution.py:29
  28.1 4.6 %collective-permute-start.6 = (f32[8,1,8,128]{3,0,2,1:T(8,128)S(1)}, f32[8,1,8,128]{3,0,2,1:T(8,128)S(1)}, u32[]{:S(2)}, u32[]{:S(2)}) collective-permute-start(f32[8,1,8,128]{3,0,2,1:T(8,128)S(1)} %copy.53), channel_id=1, source_target_pairs={{0,2},{2,4},{4,6},{6,8},{8,10},{10,12},{12,14},{14,16},{16,18},{18... | collective-permute-start | bytes 98312 | tf_op jit(solution)/shard_map/ppermute | solution.py:28
  36.9 5.6 %collective-permute-start.9 = (f32[8,4,1,128]{3,0,2,1:T(8,128)S(1)}, f32[8,4,1,128]{3,0,2,1:T(8,128)S(1)}, u32[]{:S(2)}, u32[]{:S(2)}) collective-permute-start(f32[8,4,1,128]{3,0,2,1:T(8,128)S(1)} %get-tuple-element.151), channel_id=1, source_target_pairs={{1,0},{3,2},{5,4},{7,6},{9,8},{11,10},{13,12},{15,14},{17,16},{19,... | collective-permute-start | bytes 49160 | tf_op jit(solution)/shard_map/ppermute | solution.py:29
  44.7 5.1 %collective-permute-start.10 = (f32[8,1,8,128]{3,0,2,1:T(8,128)S(1)}, f32[8,1,8,128]{3,0,2,1:T(8,128)S(1)}, u32[]{:S(2)}, u32[]{:S(2)}) collective-permute-start(f32[8,1,8,128]{3,0,2,1:T(8,128)S(1)} %copy.57), channel_id=1, source_target_pairs={{0,2},{2,4},{4,6},{6,8},{8,10},{10,12},{12,14},{14,16},{16,18},{18... | collective-permute-start | bytes 98312 | tf_op jit(solution)/shard_map/ppermute | solution.py:28
  48.3 4.3 %collective-permute-start.11 = (f32[8,1,8,128]{3,0,2,1:T(8,128)S(1)}, f32[8,1,8,128]{3,0,2,1:T(8,128)S(1)}, u32[]{:S(2)}, u32[]{:S(2)}) collective-permute-start(f32[8,1,8,128]{3,0,2,1:T(8,128)S(1)} %copy.57), channel_id=1, source_target_pairs={{2,0},{4,2},{6,4},{8,6},{10,8},{12,10},{14,12},{16,14},{18,16},{20... | collective-permute-start | bytes 98312 | tf_op jit(solution)/shard_map/ppermute | solution.py:29
  54.2 5.6 %collective-permute-start.13 = (f32[8,4,1,128]{3,0,2,1:T(8,128)S(1)}, f32[8,4,1,128]{3,0,2,1:T(8,128)S(1)}, u32[]{:S(2)}, u32[]{:S(2)}) collective-permute-start(f32[8,4,1,128]{3,0,2,1:T(8,128)S(1)} %get-tuple-element.149), channel_id=1, source_target_pairs={{1,0},{3,2},{5,4},{7,6},{9,8},{11,10},{13,12},{15,14},{17,16},{19,... | collective-permute-start | bytes 49160 | tf_op jit(solution)/shard_map/ppermute | solution.py:29
  62.1 5.1 %collective-permute-start.14 = (f32[8,1,8,128]{3,0,2,1:T(8,128)S(1)}, f32[8,1,8,128]{3,0,2,1:T(8,128)S(1)}, u32[]{:S(2)}, u32[]{:S(2)}) collective-permute-start(f32[8,1,8,128]{3,0,2,1:T(8,128)S(1)} %get-tuple-element.160), channel_id=1, source_target_pairs={{0,2},{2,4},{4,6},{6,8},{8,10},{10,12},{12,14},{14,16},{16,18},{18... | collective-permute-start | bytes 98312 | tf_op jit(solution)/shard_map/ppermute | solution.py:28
  65.9 4.3 %collective-permute-start.15 = (f32[8,1,8,128]{3,0,2,1:T(8,128)S(1)}, f32[8,1,8,128]{3,0,2,1:T(8,128)S(1)}, u32[]{:S(2)}, u32[]{:S(2)}) collective-permute-start(f32[8,1,8,128]{3,0,2,1:T(8,128)S(1)} %get-tuple-element.161), channel_id=1, source_target_pairs={{2,0},{4,2},{6,4},{8,6},{10,8},{12,10},{14,12},{16,14},{18,16},{20... | collective-permute-start | bytes 98312 | tf_op jit(solution)/shard_map/ppermute | solution.py:29
  71.8 5.6 %collective-permute-start.17 = (f32[8,4,1,128]{3,0,2,1:T(8,128)S(1)}, f32[8,4,1,128]{3,0,2,1:T(8,128)S(1)}, u32[]{:S(2)}, u32[]{:S(2)}) collective-permute-start(f32[8,4,1,128]{3,0,2,1:T(8,128)S(1)} %get-tuple-element.147), channel_id=1, source_target_pairs={{1,0},{3,2},{5,4},{7,6},{9,8},{11,10},{13,12},{15,14},{17,16},{19,... | collective-permute-start | bytes 49160 | tf_op jit(solution)/shard_map/ppermute | solution.py:29
  78.5 5.1 %collective-permute-start.18 = (f32[8,1,8,128]{3,0,2,1:T(8,128)S(1)}, f32[8,1,8,128]{3,0,2,1:T(8,128)S(1)}, u32[]{:S(2)}, u32[]{:S(2)}) collective-permute-start(f32[8,1,8,128]{3,0,2,1:T(8,128)S(1)} %get-tuple-element.158), channel_id=1, source_target_pairs={{0,2},{2,4},{4,6},{6,8},{8,10},{10,12},{12,14},{14,16},{16,18},{18... | collective-permute-start | bytes 98312 | tf_op jit(solution)/shard_map/ppermute | solution.py:28
  82.3 4.3 %collective-permute-start.19 = (f32[8,1,8,128]{3,0,2,1:T(8,128)S(1)}, f32[8,1,8,128]{3,0,2,1:T(8,128)S(1)}, u32[]{:S(2)}, u32[]{:S(2)}) collective-permute-start(f32[8,1,8,128]{3,0,2,1:T(8,128)S(1)} %get-tuple-element.159), channel_id=1, source_target_pairs={{2,0},{4,2},{6,4},{8,6},{10,8},{12,10},{14,12},{16,14},{18,16},{20... | collective-permute-start | bytes 98312 | tf_op jit(solution)/shard_map/ppermute | solution.py:29
  88.2 5.6 %collective-permute-start.21 = (f32[8,4,1,128]{3,0,2,1:T(8,128)S(1)}, f32[8,4,1,128]{3,0,2,1:T(8,128)S(1)}, u32[]{:S(2)}, u32[]{:S(2)}) collective-permute-start(f32[8,4,1,128]{3,0,2,1:T(8,128)S(1)} %get-tuple-element.145), channel_id=1, source_target_pairs={{1,0},{3,2},{5,4},{7,6},{9,8},{11,10},{13,12},{15,14},{17,16},{19,... | collective-permute-start | bytes 49160 | tf_op jit(solution)/shard_map/ppermute | solution.py:29
  143.4 5.6 %collective-permute-start.23 = (f32[8,1,8,128]{3,0,2,1:T(8,128)S(1)}, f32[8,1,8,128]{3,0,2,1:T(8,128)S(1)}, u32[]{:S(2)}, u32[]{:S(2)}) collective-permute-start(f32[8,1,8,128]{3,0,2,1:T(8,128)S(1)} %get-tuple-element.157), channel_id=1, source_target_pairs={{2,0},{4,2},{6,4},{8,6},{10,8},{12,10},{14,12},{16,14},{18,16},{20... | collective-permute-start | bytes 98312 | tf_op jit(solution)/shard_map/ppermute | solution.py:29
  150.9 5.6 %collective-permute-start.25 = (f32[8,4,1,128]{3,0,2,1:T(8,128)S(1)}, f32[8,4,1,128]{3,0,2,1:T(8,128)S(1)}, u32[]{:S(2)}, u32[]{:S(2)}) collective-permute-start(f32[8,4,1,128]{3,0,2,1:T(8,128)S(1)} %get-tuple-element.143), channel_id=1, source_target_pairs={{1,0},{3,2},{5,4},{7,6},{9,8},{11,10},{13,12},{15,14},{17,16},{19,... | collective-permute-start | bytes 49160 | tf_op jit(solution)/shard_map/ppermute | solution.py:29
  158.7 4.6 %collective-permute-start.26 = (f32[8,1,8,128]{3,0,2,1:T(8,128)S(1)}, f32[8,1,8,128]{3,0,2,1:T(8,128)S(1)}, u32[]{:S(2)}, u32[]{:S(2)}) collective-permute-start(f32[8,1,8,128]{3,0,2,1:T(8,128)S(1)} %copy.72), channel_id=1, source_target_pairs={{0,2},{2,4},{4,6},{6,8},{8,10},{10,12},{12,14},{14,16},{16,18},{18... | collective-permute-start | bytes 98312 | tf_op jit(solution)/shard_map/ppermute | solution.py:28
  161.8 4.5 %collective-permute-start.27 = (f32[8,1,8,128]{3,0,2,1:T(8,128)S(1)}, f32[8,1,8,128]{3,0,2,1:T(8,128)S(1)}, u32[]{:S(2)}, u32[]{:S(2)}) collective-permute-start(f32[8,1,8,128]{3,0,2,1:T(8,128)S(1)} %copy.72), channel_id=1, source_target_pairs={{2,0},{4,2},{6,4},{8,6},{10,8},{12,10},{14,12},{16,14},{18,16},{20... | collective-permute-start | bytes 98312 | tf_op jit(solution)/shard_map/ppermute | solution.py:29
  167.9 5.6 %collective-permute-start.29 = (f32[8,4,1,128]{3,0,2,1:T(8,128)S(1)}, f32[8,4,1,128]{3,0,2,1:T(8,128)S(1)}, u32[]{:S(2)}, u32[]{:S(2)}) collective-permute-start(f32[8,4,1,128]{3,0,2,1:T(8,128)S(1)} %get-tuple-element.141), channel_id=1, source_target_pairs={{1,0},{3,2},{5,4},{7,6},{9,8},{11,10},{13,12},{15,14},{17,16},{19,... | collective-permute-start | bytes 49160 | tf_op jit(solution)/shard_map/ppermute | solution.py:29
  175.7 5.2 %collective-permute-start.30 = (f32[8,1,8,128]{3,0,2,1:T(8,128)S(1)}, f32[8,1,8,128]{3,0,2,1:T(8,128)S(1)}, u32[]{:S(2)}, u32[]{:S(2)}) collective-permute-start(f32[8,1,8,128]{3,0,2,1:T(8,128)S(1)} %copy.76), channel_id=1, source_target_pairs={{0,2},{2,4},{4,6},{6,8},{8,10},{10,12},{12,14},{14,16},{16,18},{18... | collective-permute-start | bytes 98312 | tf_op jit(solution)/shard_map/ppermute | solution.py:28
  185.4 5.6 %collective-permute-start.33 = (f32[8,4,1,128]{3,0,2,1:T(8,128)S(1)}, f32[8,4,1,128]{3,0,2,1:T(8,128)S(1)}, u32[]{:S(2)}, u32[]{:S(2)}) collective-permute-start(f32[8,4,1,128]{3,0,2,1:T(8,128)S(1)} %get-tuple-element.139), channel_id=1, source_target_pairs={{1,0},{3,2},{5,4},{7,6},{9,8},{11,10},{13,12},{15,14},{17,16},{19,... | collective-permute-start | bytes 49160 | tf_op jit(solution)/shard_map/ppermute | solution.py:29
  193.2 5.1 %collective-permute-start.34 = (f32[8,1,8,128]{3,0,2,1:T(8,128)S(1)}, f32[8,1,8,128]{3,0,2,1:T(8,128)S(1)}, u32[]{:S(2)}, u32[]{:S(2)}) collective-permute-start(f32[8,1,8,128]{3,0,2,1:T(8,128)S(1)} %get-tuple-element.154), channel_id=1, source_target_pairs={{0,2},{2,4},{4,6},{6,8},{8,10},{10,12},{12,14},{14,16},{16,18},{18... | collective-permute-start | bytes 98312 | tf_op jit(solution)/shard_map/ppermute | solution.py:28
  201.3 4.4 %collective-permute-start.36 = (f32[8,4,1,128]{3,0,2,1:T(8,128)S(1)}, f32[8,4,1,128]{3,0,2,1:T(8,128)S(1)}, u32[]{:S(2)}, u32[]{:S(2)}) collective-permute-start(f32[8,4,1,128]{3,0,2,1:T(8,128)S(1)} %get-tuple-element.136), channel_id=1, source_target_pairs={{0,1},{2,3},{4,5},{6,7},{8,9},{10,11},{12,13},{14,15},{16,17},{18,... | collective-permute-start | bytes 49160 | tf_op jit(solution)/shard_map/ppermute | solution.py:28
  202.9 5.6 %collective-permute-start.37 = (f32[8,4,1,128]{3,0,2,1:T(8,128)S(1)}, f32[8,4,1,128]{3,0,2,1:T(8,128)S(1)}, u32[]{:S(2)}, u32[]{:S(2)}) collective-permute-start(f32[8,4,1,128]{3,0,2,1:T(8,128)S(1)} %get-tuple-element.137), channel_id=1, source_target_pairs={{1,0},{3,2},{5,4},{7,6},{9,8},{11,10},{13,12},{15,14},{17,16},{19,... | collective-permute-start | bytes 49160 | tf_op jit(solution)/shard_map/ppermute | solution.py:29
  (16 other events, 53.7 us)
where the time goes:
time: 255 us; the launch traced here: 254 us
  blocking collectives  86.6 us (34%)
  starting transfers between devices  71 us (28%)
  waiting for transfers between devices  69.9 us (27%)
  other arithmetic  14.5 us (6%)
  local copies, waits for them, and re-layouts  8.8 us (3%)
    ppermute x18, waiting for transfers between devices, with_halo(): after = lax.ppermute(first, axis, down)  62.9 us
    ppermute x18, starting transfers between devices, with_halo(): before = lax.ppermute(last, axis, up)  44.8 us
    psum x1, blocking collectives, local(): lax.psum((inner_block(first_prec, applied), inner_block(first_prec, rhs))...  43.5 us
    psum x1, blocking collectives, local(): coupling = lax.psum(inner_block(applied, next_prec), ('gx', 'gy'))  43.1 us
    ppermute x18, starting transfers between devices, with_halo(): after = lax.ppermute(first, axis, down)  23.4 us
    ppermute x2, waiting for transfers between devices, passed_along(): return lax.ppermute(shard, axis, pairs)  6.23 us
  transfers between devices with their start and end apart: 38, of which 26 were waited for; matrix products, arithmetic and copies ran while one was open for 1% of the time, Pallas kernels for 0%

commit v1 on v0

v1 whole, which is shorter than its diff:
```python
import functools

import jax
import jax.numpy as jnp
from jax import lax
from jax.experimental import pallas as pl
from jax.experimental.pallas import tpu as pltpu
from jax.sharding import PartitionSpec as P

SPRING = 8.0
OMEGA = 0.6
DAMP = 0.5
HALO = 2

MESH = pl.DeviceIdType.MESH
EXACT = lax.Precision.HIGHEST


def axis_ids(shape, dim):
    return lax.broadcasted_iota(jnp.int32, shape, dim)


def before(u, dim):
    return jnp.where(axis_ids(u.shape, dim) == 0, 0.0, pltpu.roll(u, 1, dim))


def after(u, dim):
    size = u.shape[dim]
    return jnp.where(axis_ids(u.shape, dim) == size - 1, 0.0, pltpu.roll(u, size - 1, dim))


def pair_sum(u, dim):
    size = u.shape[dim]
    even = axis_ids(u.shape, dim) % 2 == 0
    return u + jnp.where(even, pltpu.roll(u, size - 1, dim), pltpu.roll(u, 1, dim))


def block_sum(u):
    planes, rows, lanes = u.shape
    pairs = u.reshape(planes // 2, 2, rows, lanes)
    return pair_sum(pair_sum(pairs[:, 0] + pairs[:, 1], 1), 2)


def spread(c):
    cells, rows, lanes = c.shape
    return jnp.broadcast_to(c[:, None], (cells, 2, rows, lanes)).reshape(2 * cells, rows, lanes)


def hex_apply(u, e1, e2, e3):
    back = before(u, 2)
    s, d = u + back, u - back
    sb, db = before(s, 1), before(d, 1)
    ss, ds, sd, dd = s + sb, s - sb, d + db, d - db
    m00 = e1 * (ss[1:] - ss[:-1])
    s10, d10 = e1 * (ds[1:] + ds[:-1]), e2 * (ds[1:] - ds[:-1])
    s01, d01 = e1 * (sd[1:] + sd[:-1]), e2 * (sd[1:] - sd[:-1])
    s11, d11 = e2 * (dd[1:] + dd[:-1]), e3 * (dd[1:] - dd[:-1])
    t00 = m00[:-1] - m00[1:]
    t10 = (s10 + d10)[:-1] + (s10 - d10)[1:]
    t01 = (s01 + d01)[:-1] + (s01 - d01)[1:]
    t11 = (s11 + d11)[:-1] + (s11 - d11)[1:]
    ts = (t00 + t10) + after(t00 - t10, 1)
    td = (t01 + t11) + after(t01 - t11, 1)
    return (ts + td) + after(ts - td, 2)


def kernel(
    ngx, ngy,
    rhs_ref, classes_ref, supports_ref, sol_ref, res_ref, dir_ref,
    mine, cext, rext, scales, weight, spring, cstep,
    own_c, halo_c, halo_a, fields, returned, part, first_sums, group_sum, last_sums,
    gc_send, gc_recv, gr_send, gr_recv, x_send, x_recv, b_send, b_recv, a_send, a_recv, q_send, q_recv,
):
    count, lx, ly, nz = rhs_ref.shape
    group = count // ngy
    groups = ngx // group
    slots = group + 2 * HALO
    rows = ngy * ly
    planes = 2 * slots
    gx, gy = lax.axis_index("gx"), lax.axis_index("gy")
    g, s = gx // group, gx % group
    me = s * ngy + gy

    def member(at_group, j):
        return (at_group * group + j // ngy, j % ngy)

    def exists(at_group):
        return jnp.logical_and(at_group >= 0, at_group < groups)

    def guarded(condition, action):
        pl.when(condition)(action)

    barrier = pltpu.get_barrier_semaphore()

    def greet(target):
        pl.semaphore_signal(barrier, inc=1, device_id=target, device_id_type=MESH)

    for j in range(count):
        for dg in (-1, 0, 1):
            ok = exists(g + dg) if dg else j != me
            guarded(ok, functools.partial(greet, member(g + dg, j)))
    for q in range(groups):
        guarded(jnp.abs(q - g) > 1, functools.partial(greet, (q * group + s, gy)))
    below, above = (g > 0).astype(jnp.int32), (g < groups - 1).astype(jnp.int32)
    expected = (count - 1) + count * (below + above) + (groups - 1 - below - above)

    density = (classes_ref[...].astype(jnp.float32) + 1.0) / 4.0
    mine[0] = 0.001 + density * density * density
    mine[1] = supports_ref[...].astype(jnp.float32)

    def clear_below():
        cext[:, 0:HALO] = jnp.zeros((2, HALO, 2, ngy, ly, nz), jnp.float32)
        rext[0:HALO] = jnp.zeros((HALO, 2, ngy, ly, nz), jnp.float32)
        for call in range(2):
            halo_c[call, 0] = jnp.zeros((HALO, rows, nz), jnp.float32)
        halo_a[0] = jnp.zeros((2, 2, ngy, ly, nz), jnp.float32)

    def clear_above():
        cext[:, slots - HALO :] = jnp.zeros((2, HALO, 2, ngy, ly, nz), jnp.float32)
        rext[slots - HALO :] = jnp.zeros((HALO, 2, ngy, ly, nz), jnp.float32)
        for call in range(2):
            halo_c[call, 1] = jnp.zeros((HALO, rows, nz), jnp.float32)
        halo_a[1] = jnp.zeros((2, 2, ngy, ly, nz), jnp.float32)

    guarded(g == 0, clear_below)
    guarded(g == groups - 1, clear_above)
    pl.semaphore_wait(barrier, expected)

    def coef_copy(dg, j):
        slot = s + HALO - dg * group
        return pltpu.make_async_remote_copy(
            src_ref=mine, dst_ref=cext.at[:, slot, :, gy],
            send_sem=gc_send.at[dg + 1, j], recv_sem=gc_recv.at[slot, gy],
            device_id=member(g + dg, j), device_id_type=MESH)

    def rhs_copy(dg, j):
        slot = s + HALO - dg * group
        return pltpu.make_async_remote_copy(
            src_ref=rhs_ref.at[j], dst_ref=rext.at[slot, :, gy],
            send_sem=gr_send.at[dg + 1, j], recv_sem=gr_recv.at[slot, gy],
            device_id=member(g + dg, j), device_id_type=MESH)

    def sends(dg, j):
        if dg == 0:
            return j != me
        slot = s + HALO - dg * group
        return exists(g + dg) & (slot >= 0) & (slot < slots)

    for make in (coef_copy, rhs_copy):
        for dg in (-1, 1, 0):
            for j in range(count):
                guarded(sends(dg, j), lambda: make(dg, j).start())
    cext[:, s + HALO, :, gy] = mine[...]
    rext[s + HALO, :, gy] = rhs_ref[me]

    def arrives(slot, y):
        from_group = g + (slot - HALO) // group
        if HALO <= slot < HALO + group:
            return (slot - HALO) * ngy + y != me
        return exists(from_group)

    def wait_coef(slot, y):
        pltpu.make_async_remote_copy(
            src_ref=mine, dst_ref=cext.at[:, slot, :, y], send_sem=gc_send.at[0, 0],
            recv_sem=gc_recv.at[slot, y], device_id=(gx, gy), device_id_type=MESH).wait_recv()

    def wait_rhs(slot, y):
        pltpu.make_async_remote_copy(
            src_ref=rhs_ref.at[0], dst_ref=rext.at[slot, :, y], send_sem=gr_send.at[0, 0],
            recv_sem=gr_recv.at[slot, y], device_id=(gx, gy), device_id_type=MESH).wait_recv()

    for slot in range(slots):
        for y in range(ngy):
            guarded(arrives(slot, y), functools.partial(wait_coef, slot, y))

    lo, hi = 2 * HALO, planes - 2 * HALO
    plane = axis_ids((planes, rows, nz), 0) + (2 * group * g - 2 * HALO)
    inside = (plane >= 0) & (plane < ngx * lx)
    e = jnp.where(inside, cext[0].reshape(planes, rows, nz), 0.0)
    scales[0] = e * (1.0 / 16.0)
    scales[1] = e * (1.0 / 24.0)
    scales[2] = e * (1.0 / 48.0)
    spring[...] = SPRING * cext[1].reshape(planes, rows, nz)
    around = e[:-1] + e[1:]
    around = around + after(around, 1)
    around = around + after(around, 2)
    diagonal = around * (1.0 / 3.0) + spring[0 : planes - 1]
    real = inside[:-1]
    weight[0 : planes - 1] = jnp.where(real, OMEGA / jnp.where(real, diagonal, 1.0), 0.0)
    sums = block_sum(jnp.where(real, diagonal, 0.0)[lo - 2 : hi + 2])
    cstep[...] = jnp.where(sums > 0.0, DAMP / jnp.where(sums > 0.0, sums, 1.0), 0.0)

    def apply(u, start, stop):
        product = hex_apply(u, scales[0, start : stop + 1], scales[1, start : stop + 1], scales[2, start : stop + 1])
        return product + spring[start:stop] * u[1:-1]

    def swap_edges(low_src, high_src, low_dst, high_dst, k):
        down = pltpu.make_async_remote_copy(
            src_ref=low_src, dst_ref=high_dst, send_sem=x_send.at[k, 0], recv_sem=x_recv.at[k, 1],
            device_id=(jnp.maximum(gx - group, 0), gy), device_id_type=MESH)
        up = pltpu.make_async_remote_copy(
            src_ref=high_src, dst_ref=low_dst, send_sem=x_send.at[k, 1], recv_sem=x_recv.at[k, 0],
            device_id=(jnp.minimum(gx + group, ngx - 1), gy), device_id_type=MESH)
        guarded(g > 0, down.start)
        guarded(g < groups - 1, up.start)
        return down, up

    def finish_edges(down, up):
        guarded(g > 0, up.wait_recv)
        guarded(g < groups - 1, down.wait_recv)

    def drain_edges(down, up):
        guarded(g > 0, down.wait_send)
        guarded(g < groups - 1, up.wait_send)

    pending = []

    def corrected(source, call):
        z = source * weight[lo - 3 : hi + 3]
        rest = block_sum(source[1:-1] - apply(z, lo - 2, hi + 2))
        c = cstep[...] * rest
        fixed = block_sum(apply(spread(c)[1:-1], lo, hi))
        own_c[call] = c[1:-1] + cstep[1 : group + 1] * (rest[1:-1] - fixed)
        copies = swap_edges(
            own_c.at[call, pl.ds(0, HALO)], own_c.at[call, pl.ds(group - HALO, HALO)],
            halo_c.at[call, 0], halo_c.at[call, 1], call)
        pending.append(copies)
        finish_edges(*copies)
        c = jnp.concatenate([halo_c[call, 0], own_c[call], halo_c[call, 1]], axis=0)
        c = c[1:-1] + cstep[...] * (rest - block_sum(apply(spread(c)[1:-1], lo - 2, hi + 2)))
        return z[1:-1] + spread(c)

    for slot in range(slots):
        for y in range(ngy):
            guarded(arrives(slot, y), functools.partial(wait_rhs, slot, y))
    source = rext[...].reshape(planes, rows, nz)[lo - 3 : hi + 3]
    z = corrected(source, 0)
    first = z[1:-1] + weight[lo - 1 : hi + 1] * (source[2:-2] - apply(z, lo - 1, hi + 1))
    applied = apply(first, lo, hi)

    def shaped(u):
        return u.reshape(group, 2, ngy, ly, nz)

    fields[0] = shaped(first[1:-1])
    fields[1] = shaped(applied)
    own_a = fields.at[1]
    halo_src_low = own_a.at[pl.ds(0, 2)]
    halo_src_high = own_a.at[pl.ds(group - 2, 2)]
    copies = swap_edges(halo_src_low, halo_src_high, halo_a.at[0], halo_a.at[1], 2)
    pending.append(copies)

    def back_copy(k, f, n, j):
        return pltpu.make_async_remote_copy(
            src_ref=fields.at[pl.ds(f, n), j // ngy, :, j % ngy], dst_ref=returned.at[pl.ds(f, n), me],
            send_sem=b_send.at[k, j], recv_sem=b_recv.at[k, me],
            device_id=member(g, j), device_id_type=MESH)

    def wait_back(k, f, n, j):
        pltpu.make_async_remote_copy(
            src_ref=fields.at[pl.ds(f, n), 0, :, 0], dst_ref=returned.at[pl.ds(f, n), j],
            send_sem=b_send.at[k, j], recv_sem=b_recv.at[k, j],
            device_id=(gx, gy), device_id_type=MESH).wait_recv()

    def send_back(k, f, n):
        for j in range(count):
            guarded(j != me, lambda: back_copy(k, f, n, j).start())
        for i in range(f, f + n):
            returned[i, me] = fields[i, s, :, gy]

    send_back(0, 0, 2)
    finish_edges(*copies)
    low = halo_a[0].reshape(4, rows, nz)[1:]
    high = halo_a[1].reshape(4, rows, nz)[:-1]
    source = jnp.concatenate([low, applied, high], axis=0)
    z = corrected(source, 1)[1:-1]
    own = slice(lo, hi)
    fields[2] = shaped(z[1:-1] + weight[own] * (applied - apply(z, lo, hi)))
    send_back(1, 2, 1)
    for k, f, n in ((0, 0, 2), (1, 2, 1)):
        for j in range(count):
            guarded(j != me, functools.partial(wait_back, k, f, n, j))

    def flat(block):
        parts = []
        for a in range(lx):
            turned = jnp.swapaxes(block[:, a], 0, 1)
            parts += [turned[b] for b in range(ly)]
        return jnp.concatenate(parts, axis=1)

    field, product, twice = flat(returned[0]), flat(returned[1]), flat(returned[2])
    given = flat(rhs_ref[...])
    none = jnp.zeros_like(field)
    left = jnp.concatenate([field, product], axis=1)
    right = jnp.concatenate([
        jnp.concatenate([product, field], axis=1),
        jnp.concatenate([given, none], axis=1),
        jnp.concatenate([none, field], axis=1),
        jnp.concatenate([none, twice], axis=1),
        jnp.zeros((128 - 4 * count, 2 * field.shape[1]), jnp.float32)], axis=0)
    part[...] = lax.dot_general(
        left, right, (((1,), (1,)), ((), ())), precision=EXACT, preferred_element_type=jnp.float32)

    def sum_copy(j):
        return pltpu.make_async_remote_copy(
            src_ref=part, dst_ref=first_sums.at[me], send_sem=a_send.at[j], recv_sem=a_recv.at[me],
            device_id=member(g, j), device_id_type=MESH)

    def sum_wait(j):
        pltpu.make_async_remote_copy(
            src_ref=part, dst_ref=first_sums.at[j], send_sem=a_send.at[j], recv_sem=a_recv.at[j],
            device_id=(gx, gy), device_id_type=MESH).wait_recv()

    for j in range(count):
        guarded(j != me, lambda: sum_copy(j).start())
    first_sums[me] = part[...]
    for j in range(count):
        guarded(j != me, functools.partial(sum_wait, j))
    group_sum[...] = jnp.sum(first_sums[...], axis=0)

    def total_copy(q):
        return pltpu.make_async_remote_copy(
            src_ref=group_sum, dst_ref=last_sums.at[g], send_sem=q_send.at[q], recv_sem=q_recv.at[g],
            device_id=(q * group + s, gy), device_id_type=MESH)

    def total_wait(q):
        pltpu.make_async_remote_copy(
            src_ref=group_sum, dst_ref=last_sums.at[q], send_sem=q_send.at[q], recv_sem=q_recv.at[q],
            device_id=(gx, gy), device_id_type=MESH).wait_recv()

    for q in range(groups):
        guarded(q != g, lambda: total_copy(q).start())
    last_sums[g] = group_sum[...]
    for q in range(groups):
        guarded(q != g, functools.partial(total_wait, q))
    system = jnp.sum(last_sums[...], axis=0)

    lane = axis_ids(system.shape, 1)
    row = axis_ids(system.shape, 0)
    system = jnp.where(lane < count, 0.5 * system, system)
    for k in range(count):
        column = jnp.sum(jnp.where(lane == k, system, 0.0), axis=1, keepdims=True)
        pivot_row = system[k : k + 1]
        scaled = pivot_row / pivot_row[:, k : k + 1]
        system = jnp.where(row == k, scaled, system - column * scaled)

    def columns(n):
        return system[:, n * count : (n + 1) * count]

    step = columns(1)
    turn = jnp.dot(columns(3), step, precision=EXACT, preferred_element_type=jnp.float32) - columns(2)

    def mixed(coef, u):
        return lax.dot_general(
            coef, u, (((0,), (0,)), ((), ())), precision=EXACT, preferred_element_type=jnp.float32)

    def put(ref, u):
        for a in range(lx):
            at = a * ly
            block = jnp.stack([u[:, (at + b) * nz : (at + b + 1) * nz] for b in range(ly)], axis=0)
            ref[:, a] = jnp.swapaxes(block, 0, 1)

    put(sol_ref, mixed(step, field))
    put(res_ref, given - mixed(step, product))
    put(dir_ref, field + mixed(turn, field) - mixed(step, twice))

    for make in (coef_copy, rhs_copy):
        for dg in (-1, 1, 0):
            for j in range(count):
                guarded(sends(dg, j), lambda: make(dg, j).wait_send())
    for copies in pending:
        drain_edges(*copies)
    for k, f, n in ((0, 0, 2), (1, 2, 1)):
        for j in range(count):
            guarded(j != me, lambda: back_copy(k, f, n, j).wait_send())
    for j in range(count):
        guarded(j != me, lambda: sum_copy(j).wait_send())
    for q in range(groups):
        guarded(q != g, lambda: total_copy(q).wait_send())


def local(ngx, ngy, rhs, classes, supports):
    count, lx, ly, nz = rhs.shape
    group = count // ngy
    groups = ngx // group
    slots = group + 2 * HALO
    rows = ngy * ly
    planes = 2 * slots
    f32 = jnp.float32
    dma = pltpu.SemaphoreType.DMA
    return pl.pallas_call(
        functools.partial(kernel, ngx, ngy),
        out_shape=[jax.ShapeDtypeStruct(rhs.shape, f32)] * 3,
        in_specs=[pl.BlockSpec(memory_space=pltpu.VMEM)] * 3,
        out_specs=[pl.BlockSpec(memory_space=pltpu.VMEM)] * 3,
        scratch_shapes=[
            pltpu.VMEM((2, lx, ly, nz), f32),
            pltpu.VMEM((2, slots, 2, ngy, ly, nz), f32),
            pltpu.VMEM((slots, 2, ngy, ly, nz), f32),
            pltpu.VMEM((3, planes, rows, nz), f32),
            pltpu.VMEM((planes, rows, nz), f32),
            pltpu.VMEM((planes, rows, nz), f32),
            pltpu.VMEM((group + 2, rows, nz), f32),
            pltpu.VMEM((2, group, rows, nz), f32),
            pltpu.VMEM((2, 2, HALO, rows, nz), f32),
            pltpu.VMEM((2, 2, 2, ngy, ly, nz), f32),
            pltpu.VMEM((3, group, 2, ngy, ly, nz), f32),
            pltpu.VMEM((3, count, lx, ly, nz), f32),
            pltpu.VMEM((count, 128), f32),
            pltpu.VMEM((count, count, 128), f32),
            pltpu.VMEM((count, 128), f32),
            pltpu.VMEM((groups, count, 128), f32),
            dma((3, count)), dma((slots, ngy)), dma((3, count)), dma((slots, ngy)),
            dma((3, 2)), dma((3, 2)), dma((2, count)), dma((2, count)),
            dma((count,)), dma((count,)), dma((groups,)), dma((groups,)),
        ],
        compiler_params=pltpu.CompilerParams(
            collective_id=0, has_side_effects=True, vmem_limit_bytes=32 * 1024 * 1024),
        name="block_step",
    )(rhs, classes, supports)


def solution(mesh):
    ngx, ngy = mesh.shape["gx"], mesh.shape["gy"]
    spread_out = P(None, "gx", "gy", None)
    return jax.shard_map(
        functools.partial(local, ngx, ngy),
        mesh=mesh,
        in_specs=(spread_out, P("gx", "gy", None), P("gx", "gy", None)),
        out_specs=(spread_out, spread_out, spread_out),
        check_vma=False,
    )
```

time: 255 us -> 41.8 us (0.16)
  blocking collectives: 86.6 us -> 0 us
  starting transfers between devices: 71 us -> 0 us
  waiting for transfers between devices: 69.9 us -> 0 us
  Pallas kernels: 0 us -> 36.8 us
  other arithmetic: 14.5 us -> 0 us
  local copies, waits for them, and re-layouts: 8.8 us -> 4.12 us
    psum x2 -> x0, blocking collectives: 86.6 us -> none  [the longest x1 43.5 us: local(): lax.psum((inner_block(first_prec, applied), inner_block(first_prec, rhs))...]
    ppermute x38 -> x0, starting transfers between devices: 71 us -> none  [the longest x18 44.8 us: with_halo(): before = lax.ppermute(last, axis, up)]
    ppermute x38 -> x0, waiting for transfers between devices: 69.9 us -> none  [the longest x18 62.9 us: with_halo(): after = lax.ppermute(first, axis, down)]
    pallas_call x0 -> x1, Pallas kernels: none -> 36.8 us  [local(): pl.pallas_call(functools.partial(kernel, ngx, ngy), out_shape=[jax.ShapeD...]
    reduce_sum x13 -> x0, other arithmetic: 5 us -> none  [restrict(): return field.reshape(k, a // 2, 2, b // 2, 2, c // 2, 2).sum(axis=(2, 4, 6))]
    slice x20 -> x0, other arithmetic: 2.81 us -> none  [the longest x9 2.68 us: hex_product(): corners[a, b, c] = padded[..., a:a + nx + 1, b:b + ny + 1, c:c + nz + 1]]
    slice x19 -> x0, local copies, waits for them, and re-layouts: 2.81 us -> none  [the longest x9 2.13 us: hex_product(): corners[a, b, c] = padded[..., a:a + nx + 1, b:b + ny + 1, c:c + nz + 1]]
    another operation x5 -> x0, other arithmetic: 2.67 us -> none  [the longest x3 1.39 us: spd_solve(): lower = jnp.linalg.cholesky(matrix)]
  transfers between devices with their start and end apart: 38 -> 0, of which waited for: 26 -> 0; matrix products, arithmetic and copies ran while one was open for 1% -> 0% of each run, Pallas kernels for 0% -> 0%
where the time goes in v1:
time: 41.8 us; the launch traced here: 41.5 us
  Pallas kernels  36.8 us (88%)
  local copies, waits for them, and re-layouts  4.12 us (10%)
  between operations  0.65 us (2%)
    pallas_call x1, Pallas kernels, local(): pl.pallas_call(functools.partial(kernel, ngx, ngy), out_shape=[jax.ShapeD...  36.8 us
    unnamed x9, local copies, waits for them, and re-layouts  4.12 us

profile of v1, /device:TPU:0, one launch (start us, length us, event | category | flops | bytes accessed | tf_op | source)
XLA Modules:
  0.0 41.5 jit_solution(5338636314290217168)
XLA Ops:
  0.6 0.0 copy-start
  0.6 0.8 %copy-done = f32[8,2,8,128]{3,2,1,0:T(8,128)S(1)} copy-done((f32[8,2,8,128]{3,2,1,0:T(8,128)S(1)}, f32[8,2,8,128]{3,2,1,0:T(8,128)}, u32[]{:S(2)}) %copy-start) | copy-done | bytes 65560
  1.5 0.0 copy-start.1
  1.5 0.7 %copy-done.1 = s32[2,8,128]{2,1,0:T(8,128)S(1)} copy-done((s32[2,8,128]{2,1,0:T(8,128)S(1)}, s32[2,8,128]{2,1,0:T(8,128)}, u32[]{:S(2)}) %copy-start.1) | copy-done | bytes 8216
  2.2 0.0 copy-start.2
  2.2 0.7 %copy-done.2 = s32[2,8,128]{2,1,0:T(8,128)S(1)} copy-done((s32[2,8,128]{2,1,0:T(8,128)S(1)}, s32[2,8,128]{2,1,0:T(8,128)}, u32[]{:S(2)}) %copy-start.2) | copy-done | bytes 8216
  2.9 36.8 %block_step.1 = (f32[8,2,8,128]{3,2,1,0:T(8,128)S(1)}, f32[8,2,8,128]{3,2,1,0:T(8,128)S(1)}, f32[8,2,8,128]{3,2,1,0:T(8,128)S(1)}) custom-call(f32[8,2,8,128]{3,2,1,0:T(8,128)S(1)} %copy-done, s32[2,8,128]{2,1,0:T(8,128)S(1)} %copy-done.1, s32[2,8,128]{2,1,0:T(8,128)S(1)} %copy-done.2), custom_call_target="tpu_custom_call" | custom-call | tf_op jit(solution)/shard_map/block_step/pallas_call | solution.py:390
  39.7 0.6 %copy.9 = f32[8,2,8,128]{3,2,1,0:T(8,128)} copy(f32[8,2,8,128]{3,2,1,0:T(8,128)S(1)} %get-tuple-element.6) | data formatting | bytes 131072
  40.3 0.6 %copy.10 = f32[8,2,8,128]{3,2,1,0:T(8,128)} copy(f32[8,2,8,128]{3,2,1,0:T(8,128)S(1)} %get-tuple-element.7) | data formatting | bytes 131072
  40.9 0.6 %copy.11 = f32[8,2,8,128]{3,2,1,0:T(8,128)} copy(f32[8,2,8,128]{3,2,1,0:T(8,128)S(1)} %get-tuple-element.8) | data formatting | bytes 131072
Async XLA Ops:
  0.6 0.8 %copy-start = (f32[8,2,8,128]{3,2,1,0:T(8,128)S(1)}, f32[8,2,8,128]{3,2,1,0:T(8,128)}, u32[]{:S(2)}) copy-start(f32[8,2,8,128]{3,2,1,0:T(8,128)} %rhs_ref.1) | copy-start | bytes 196612
  1.5 0.7 %copy-start.1 = (s32[2,8,128]{2,1,0:T(8,128)S(1)}, s32[2,8,128]{2,1,0:T(8,128)}, u32[]{:S(2)}) copy-start(s32[2,8,128]{2,1,0:T(8,128)} %classes_ref.1) | copy-start | bytes 24580
  2.2 0.7 %copy-start.2 = (s32[2,8,128]{2,1,0:T(8,128)S(1)}, s32[2,8,128]{2,1,0:T(8,128)}, u32[]{:S(2)}) copy-start(s32[2,8,128]{2,1,0:T(8,128)} %supports_ref.1) | copy-start | bytes 24580

commit v2 on v1

v2 whole, which is shorter than its diff:
```python
import functools

import jax
import jax.numpy as jnp
from jax import lax
from jax.experimental import pallas as pl
from jax.experimental.pallas import tpu as pltpu
from jax.sharding import PartitionSpec as P

SPRING = 8.0
OMEGA = 0.6
DAMP = 0.5
HALO = 2

MESH = pl.DeviceIdType.MESH
EXACT = lax.Precision.HIGHEST


def axis_ids(shape, dim):
    return lax.broadcasted_iota(jnp.int32, shape, dim)


def once(f):
    return functools.cache(f)


def halves(u):
    top = u.astype(jnp.bfloat16)
    return top, (u - top.astype(jnp.float32)).astype(jnp.bfloat16)


def kernel(
    ngx, ngy,
    rhs_hbm, classes_hbm, supports_hbm, sol_ref, res_ref, dir_ref,
    rhs_ref, classes_ref, supports_ref,
    mine, cext, rext, scales, weight, spring, cstep, rest, coarse, smooth, first,
    own_c, halo_c, halo_a, fields, returned, part, first_sums, group_sum, last_sums,
    in_sem, gc_send, gc_recv, gr_send, gr_recv, x_send, x_recv, b_send, b_recv, a_send, a_recv, q_send, q_recv,
):
    count, lx, ly, nz = rhs_ref.shape
    group = count // ngy
    groups = ngx // group
    slots = group + 2 * HALO
    rows = ngy * ly
    planes = 2 * slots
    gx, gy = lax.axis_index("gx"), lax.axis_index("gy")
    g, s = gx // group, gx % group
    me = s * ngy + gy
    others = [(me + o) % count for o in range(1, count)]
    other_groups = [(g + o) % groups for o in range(1, groups)]

    loads = [
        pltpu.make_async_copy(classes_hbm, classes_ref, in_sem.at[0]),
        pltpu.make_async_copy(supports_hbm, supports_ref, in_sem.at[1]),
        pltpu.make_async_copy(rhs_hbm, rhs_ref, in_sem.at[2]),
    ]
    for load in loads:
        load.start()

    def member(at_group, j):
        return (at_group * group + j // ngy, j % ngy)

    barrier = pltpu.get_barrier_semaphore()

    def greet(target):
        pl.semaphore_signal(barrier, inc=1, device_id=target, device_id_type=MESH)

    def greet_group(at_group):
        for j in range(count):
            greet(member(at_group, j))

    has_below, has_above = g > 0, g < groups - 1
    for j in others:
        greet(member(g, j))
    pl.when(has_below)(lambda: greet_group(g - 1))
    pl.when(has_above)(lambda: greet_group(g + 1))
    for q in range(groups):
        pl.when(jnp.abs(q - g) > 1)(functools.partial(greet, (q * group + s, gy)))
    below, above = has_below.astype(jnp.int32), has_above.astype(jnp.int32)
    expected = (count - 1) + count * (below + above) + (groups - 1 - below - above)

    def clear(side):
        at = 0 if side == 0 else slots - HALO
        cext[:, at : at + HALO] = jnp.zeros((2, HALO, 2, ngy, ly, nz), jnp.float32)
        rext[at : at + HALO] = jnp.zeros((HALO, 2, ngy, ly, nz), jnp.float32)
        for call in range(2):
            halo_c[call, side] = jnp.zeros((HALO, rows, nz), jnp.float32)
        halo_a[side] = jnp.zeros((2, 2, ngy, ly, nz), jnp.float32)

    pl.when(g == 0)(lambda: clear(0))
    pl.when(g == groups - 1)(lambda: clear(1))
    loads[0].wait()
    density = (classes_ref[...].astype(jnp.float32) + 1.0) / 4.0
    mine[0] = 0.001 + density * density * density
    loads[1].wait()
    mine[1] = supports_ref[...].astype(jnp.float32)
    loads[2].wait()
    pl.semaphore_wait(barrier, expected)

    def coef_copy(dg, j):
        slot = s + HALO - dg * group
        return pltpu.make_async_remote_copy(
            src_ref=mine, dst_ref=cext.at[:, slot, :, gy],
            send_sem=gc_send.at[dg + 1, j], recv_sem=gc_recv.at[slot, gy],
            device_id=member(g + dg, j), device_id_type=MESH)

    def rhs_copy(dg, j):
        slot = s + HALO - dg * group
        return pltpu.make_async_remote_copy(
            src_ref=rhs_ref.at[j], dst_ref=rext.at[slot, :, gy],
            send_sem=gr_send.at[dg + 1, j], recv_sem=gr_recv.at[slot, gy],
            device_id=member(g + dg, j), device_id_type=MESH)

    def outward(action):
        for dg, there in ((-1, has_below), (1, has_above)):
            slot = s + HALO - dg * group

            @pl.when(there & (slot >= 0) & (slot < slots))
            def _():
                for make in (coef_copy, rhs_copy):
                    for j in range(count):
                        action(make(dg, j))

    outward(lambda copy: copy.start())
    for make in (coef_copy, rhs_copy):
        for j in others:
            make(0, j).start()
    cext[:, s + HALO, :, gy] = mine[...]
    rext[s + HALO, :, gy] = rhs_ref[me]

    def wait_coef(slot, y):
        pltpu.make_async_remote_copy(
            src_ref=mine, dst_ref=cext.at[:, slot, :, y], send_sem=gc_send.at[0, 0],
            recv_sem=gc_recv.at[slot, y], device_id=(gx, gy), device_id_type=MESH).wait_recv()

    def wait_rhs(slot, y):
        pltpu.make_async_remote_copy(
            src_ref=rhs_ref.at[0], dst_ref=rext.at[slot, :, y], send_sem=gr_send.at[0, 0],
            recv_sem=gr_recv.at[slot, y], device_id=(gx, gy), device_id_type=MESH).wait_recv()

    def wait_all(wait):
        def side(at):
            for slot in range(at, at + HALO):
                for y in range(ngy):
                    wait(slot, y)

        for j in others:
            wait(HALO + j // ngy, j % ngy)
        pl.when(has_below)(lambda: side(0))
        pl.when(has_above)(lambda: side(HALO + group))

    shape = (rows, nz)
    row_id, lane_id = axis_ids(shape, 0), axis_ids(shape, 1)
    first_row, last_row = row_id == 0, row_id == rows - 1
    first_lane, last_lane = lane_id == 0, lane_id == nz - 1
    tiles = (rows // 8, 8, nz)
    even_row, even_lane = axis_ids(tiles, 1) % 2 == 0, lane_id % 2 == 0

    def before_y(u):
        return jnp.where(first_row, 0.0, pltpu.roll(u, 1, 0))

    def after_y(u):
        return jnp.where(last_row, 0.0, pltpu.roll(u, rows - 1, 0))

    def before_z(u):
        return jnp.where(first_lane, 0.0, pltpu.roll(u, 1, 1))

    def after_z(u):
        return jnp.where(last_lane, 0.0, pltpu.roll(u, nz - 1, 1))

    def pair_sums(u):
        t = u.reshape(tiles)
        t = t + jnp.where(even_row, pltpu.roll(t, 7, 1), pltpu.roll(t, 1, 1))
        u = t.reshape(shape)
        return u + jnp.where(even_lane, pltpu.roll(u, nz - 1, 1), pltpu.roll(u, 1, 1))

    def forward(u):
        back = before_z(u)
        a, d = u + back, u - back
        ab, db = before_y(a), before_y(d)
        return a + ab, a - ab, d + db, d - db

    def inverse(t):
        t00, t10, t01, t11 = t
        ts = (t00 + t10) + after_y(t00 - t10)
        td = (t01 + t11) + after_y(t01 - t11)
        return (ts + td) + after_z(ts - td)

    def element(low, high, i):
        e1, e2, e3 = scales[0, i], scales[1, i], scales[2, i]
        m00 = e1 * (high[0] - low[0])
        s10, d10 = e1 * (high[1] + low[1]), e2 * (high[1] - low[1])
        s01, d01 = e1 * (high[2] + low[2]), e2 * (high[2] - low[2])
        s11, d11 = e2 * (high[3] + low[3]), e3 * (high[3] - low[3])
        return (m00, s10 + d10, s01 + d01, s11 + d11), (-m00, s10 - d10, s01 - d01, s11 - d11)

    def both(low, high, i):
        e1, e2 = scales[0, i], scales[1, i]
        return e1 * (high[1] + low[1]), e1 * (high[2] + low[2]), e2 * (high[3] + low[3])

    def plane_apply(value, start, stop):
        spectrum = once(lambda p: forward(value(p)))
        parts = once(lambda i: element(spectrum(i - 1), spectrum(i), i))
        for p in range(start, stop):
            t = [u + v for u, v in zip(parts(p)[0], parts(p + 1)[1])]
            yield p, inverse(t) + spring[p] * value(p)

    def cell_sums(spectrum, start, stop):
        parts = once(lambda i: element(spectrum(i - 1), spectrum(i), i))
        for cell in range(start, stop):
            p = 2 * cell
            up, down = parts(p)[0], parts(p + 2)[1]
            mid = [2.0 * u for u in both(spectrum(p), spectrum(p + 1), p + 1)]
            t = [up[0] + down[0]] + [up[k + 1] + mid[k] + down[k + 1] for k in range(3)]
            yield cell, inverse(t)

    def coarse_sums(value, start, stop):
        spectrum = once(lambda cell: forward(value(cell)))
        for cell, total in cell_sums(lambda p: spectrum(p // 2), start, stop):
            p = 2 * cell
            yield cell, pair_sums(total + (spring[p] + spring[p + 1]) * value(cell))

    lo, hi = 2 * HALO, planes - 2 * HALO
    near = range(HALO - 1, HALO + group + 1)
    wait_all(wait_coef)

    def inside(p):
        if p < lo:
            return jnp.where(has_below, jnp.float32(1.0), jnp.float32(0.0))
        if p >= hi:
            return jnp.where(has_above, jnp.float32(1.0), jnp.float32(0.0))
        return None

    def shared(amount, value, p):
        there = inside(p)
        return amount / value if there is None else there * (amount / (value + (1.0 - there)))

    def stiff(p):
        return cext[0, p // 2, p % 2].reshape(shape)

    diagonals = {}
    for p in range(lo - 3, hi + 4):
        e = stiff(p)
        scales[0, p] = e * (1.0 / 16.0)
        scales[1, p] = e * (1.0 / 24.0)
        scales[2, p] = e * (1.0 / 48.0)
        if p < hi + 3:
            tied = SPRING * cext[1, p // 2, p % 2].reshape(shape)
            spring[p] = tied
            around = e + stiff(p + 1)
            around = around + after_y(around)
            around = around + after_z(around)
            diagonals[p] = around * (1.0 / 3.0) + tied
            weight[p] = shared(OMEGA, diagonals[p], p)
        if p % 2 and p // 2 in near:
            cstep[p // 2] = shared(DAMP, pair_sums(diagonals[p - 1] + diagonals[p]), p)

    def swap_edges(low_src, high_src, low_dst, high_dst, k):
        down = pltpu.make_async_remote_copy(
            src_ref=low_src, dst_ref=high_dst, send_sem=x_send.at[k, 0], recv_sem=x_recv.at[k, 1],
            device_id=(jnp.maximum(gx - group, 0), gy), device_id_type=MESH)
        up = pltpu.make_async_remote_copy(
            src_ref=high_src, dst_ref=low_dst, send_sem=x_send.at[k, 1], recv_sem=x_recv.at[k, 0],
            device_id=(jnp.minimum(gx + group, ngx - 1), gy), device_id_type=MESH)
        pl.when(has_below)(down.start)
        pl.when(has_above)(up.start)
        return down, up

    def finish_edges(down, up):
        pl.when(has_below)(up.wait_recv)
        pl.when(has_above)(down.wait_recv)

    def drain_edges(down, up):
        pl.when(has_below)(down.wait_send)
        pl.when(has_above)(up.wait_send)

    pending = []

    def correct(source, call):
        def z(p):
            return source(p) * weight[p]

        spectrum = once(lambda p: forward(z(p)))
        for cell, total in cell_sums(spectrum, near.start, near.stop):
            p = 2 * cell
            given = (source(p) - spring[p] * z(p)) + (source(p + 1) - spring[p + 1] * z(p + 1))
            value = pair_sums(given - total)
            rest[cell] = value
            coarse[cell] = cstep[cell] * value
        for cell, total in coarse_sums(lambda c: coarse[c], HALO, HALO + group):
            own_c[call, cell - HALO] = coarse[cell] + cstep[cell] * (rest[cell] - total)
        copies = swap_edges(
            own_c.at[call, pl.ds(0, HALO)], own_c.at[call, pl.ds(group - HALO, HALO)],
            halo_c.at[call, 0], halo_c.at[call, 1], call)
        pending.append(copies)
        finish_edges(*copies)

        def swept(cell):
            if cell < HALO:
                return halo_c[call, 0, cell]
            if cell < HALO + group:
                return own_c[call, cell - HALO]
            return halo_c[call, 1, cell - HALO - group]

        for cell, total in coarse_sums(swept, near.start, near.stop):
            c = swept(cell) + cstep[cell] * (rest[cell] - total)
            for p in (2 * cell, 2 * cell + 1):
                smooth[p] = z(p) + c

    def smoothed(source, start, stop):
        for p, product in plane_apply(lambda p: smooth[p], start, stop):
            yield p, smooth[p] + weight[p] * (source(p) - product)

    def keep(f, p, u):
        fields[f, (p - lo) // 2, (p - lo) % 2] = u.reshape(ngy, ly, nz)

    wait_all(wait_rhs)

    def given_plane(p):
        return rext[p // 2, p % 2].reshape(shape)

    correct(given_plane, 0)
    for p, u in smoothed(given_plane, lo - 1, hi + 1):
        first[p] = u
        if lo <= p < hi:
            keep(0, p, u)
    for p, u in plane_apply(lambda p: first[p], lo, hi):
        keep(1, p, u)

    copies = swap_edges(
        fields.at[1, pl.ds(0, 2)], fields.at[1, pl.ds(group - 2, 2)], halo_a.at[0], halo_a.at[1], 2)
    pending.append(copies)

    def back_copy(k, f, n, j):
        return pltpu.make_async_remote_copy(
            src_ref=fields.at[pl.ds(f, n), j // ngy, :, j % ngy], dst_ref=returned.at[pl.ds(f, n), me],
            send_sem=b_send.at[k, j], recv_sem=b_recv.at[k, me],
            device_id=member(g, j), device_id_type=MESH)

    def wait_back(k, f, n, j):
        pltpu.make_async_remote_copy(
            src_ref=fields.at[pl.ds(f, n), 0, :, 0], dst_ref=returned.at[pl.ds(f, n), j],
            send_sem=b_send.at[k, j], recv_sem=b_recv.at[k, j],
            device_id=(gx, gy), device_id_type=MESH).wait_recv()

    def send_back(k, f, n):
        for j in others:
            back_copy(k, f, n, j).start()
        for i in range(f, f + n):
            returned[i, me] = fields[i, s, :, gy]

    send_back(0, 0, 2)
    finish_edges(*copies)

    def product_plane(p):
        if p < lo:
            u = halo_a[0, p // 2, p % 2]
        elif p < hi:
            u = fields[1, (p - lo) // 2, (p - lo) % 2]
        else:
            u = halo_a[1, (p - hi) // 2, (p - hi) % 2]
        return u.reshape(shape)

    correct(product_plane, 1)
    for p, u in smoothed(product_plane, lo, hi):
        keep(2, p, u)
    send_back(1, 2, 1)

    def flat(block):
        parts = []
        for a in range(lx):
            turned = jnp.swapaxes(block[:, a], 0, 1)
            parts += [turned[b] for b in range(ly)]
        return jnp.concatenate(parts, axis=1)

    given = flat(rhs_ref[...])
    for j in others:
        wait_back(0, 0, 2, j)
    field, product = flat(returned[0]), flat(returned[1])
    for j in others:
        wait_back(1, 2, 1, j)
    twice = flat(returned[2])

    def dot(left, right, dims):
        return lax.dot_general(left, right, (dims, ((), ())), preferred_element_type=jnp.float32)

    left_top, left_low = halves(jnp.concatenate([field, product], axis=0))
    right_top, right_low = halves(jnp.concatenate([product, given, field, twice], axis=0))
    sums = dot(
        jnp.concatenate([left_top, left_low, left_top], axis=1),
        jnp.concatenate([right_top, right_top, right_low], axis=1), ((1,), (1,)))
    wide = 4 * count
    lane = axis_ids((count, wide), 1)
    part[...] = jnp.zeros_like(part)
    part[:, 0:wide] = jnp.where(lane < 2 * count, sums[:count], sums[count:])

    def sum_copy(j):
        return pltpu.make_async_remote_copy(
            src_ref=part, dst_ref=first_sums.at[me], send_sem=a_send.at[j], recv_sem=a_recv.at[me],
            device_id=member(g, j), device_id_type=MESH)

    def sum_wait(j):
        pltpu.make_async_remote_copy(
            src_ref=part, dst_ref=first_sums.at[j], send_sem=a_send.at[j], recv_sem=a_recv.at[j],
            device_id=(gx, gy), device_id_type=MESH).wait_recv()

    for j in others:
        sum_copy(j).start()
    first_sums[me] = part[...]
    for j in others:
        sum_wait(j)
    group_sum[...] = jnp.sum(first_sums[...], axis=0)

    def total_copy(q):
        return pltpu.make_async_remote_copy(
            src_ref=group_sum, dst_ref=last_sums.at[g], send_sem=q_send.at[q], recv_sem=q_recv.at[g],
            device_id=(q * group + s, gy), device_id_type=MESH)

    def total_wait(q):
        pltpu.make_async_remote_copy(
            src_ref=group_sum, dst_ref=last_sums.at[q], send_sem=q_send.at[q], recv_sem=q_recv.at[q],
            device_id=(gx, gy), device_id_type=MESH).wait_recv()

    for q in other_groups:
        total_copy(q).start()
    last_sums[g] = group_sum[...]
    for q in other_groups:
        total_wait(q)
    system = jnp.sum(last_sums[...], axis=0)

    lane = axis_ids(system.shape, 1)
    row = axis_ids(system.shape, 0)
    mirrored = pltpu.roll(system, system.shape[1] - 2 * count, 1)
    system = jnp.where(lane < count, 0.5 * (system + mirrored), system)
    for k in range(count):
        column = jnp.sum(jnp.where(lane == k, system, 0.0), axis=1, keepdims=True)
        pivot_row = system[k : k + 1]
        scaled = pivot_row / pivot_row[:, k : k + 1]
        system = jnp.where(row == k, scaled, system - column * scaled)

    def columns(n):
        return system[:, n * count : (n + 1) * count]

    step = columns(1)
    turn = jnp.dot(columns(3), step, precision=EXACT, preferred_element_type=jnp.float32) - columns(2)

    def mixed(coef, u):
        coef_top, u_top = [v.astype(jnp.bfloat16).astype(jnp.float32) for v in (coef, u)]
        coefs = jnp.concatenate([coef_top, coef - coef_top, coef_top], axis=0).astype(jnp.bfloat16)
        terms = jnp.concatenate([u_top, u_top, u - u_top], axis=0).astype(jnp.bfloat16)
        return dot(coefs, terms, ((0,), (0,)))

    def put(ref, u):
        for a in range(lx):
            at = a * ly
            block = jnp.stack([u[:, (at + b) * nz : (at + b + 1) * nz] for b in range(ly)], axis=0)
            ref[:, a] = jnp.swapaxes(block, 0, 1)

    put(sol_ref, mixed(step, field))
    put(res_ref, given - mixed(step, product))
    put(dir_ref, field + mixed(jnp.concatenate([turn, -step], axis=0), jnp.concatenate([field, twice], axis=0)))

    outward(lambda copy: copy.wait_send())
    for make in (coef_copy, rhs_copy):
        for j in others:
            make(0, j).wait_send()
    for copies in pending:
        drain_edges(*copies)
    for k, f, n in ((0, 0, 2), (1, 2, 1)):
        for j in others:
            back_copy(k, f, n, j).wait_send()
    for j in others:
        sum_copy(j).wait_send()
    for q in other_groups:
        total_copy(q).wait_send()


def local(ngx, ngy, rhs, classes, supports):
    count, lx, ly, nz = rhs.shape
    group = count // ngy
    groups = ngx // group
    slots = group + 2 * HALO
    rows = ngy * ly
    planes = 2 * slots
    f32 = jnp.float32
    dma = pltpu.SemaphoreType.DMA
    return pl.pallas_call(
        functools.partial(kernel, ngx, ngy),
        out_shape=[jax.ShapeDtypeStruct(rhs.shape, f32)] * 3,
        in_specs=[pl.BlockSpec(memory_space=pltpu.HBM)] * 3,
        out_specs=[pl.BlockSpec(memory_space=pltpu.VMEM)] * 3,
        scratch_shapes=[
            pltpu.VMEM(rhs.shape, f32),
            pltpu.VMEM(classes.shape, jnp.int32),
            pltpu.VMEM(supports.shape, jnp.int32),
            pltpu.VMEM((2, lx, ly, nz), f32),
            pltpu.VMEM((2, slots, 2, ngy, ly, nz), f32),
            pltpu.VMEM((slots, 2, ngy, ly, nz), f32),
            pltpu.VMEM((3, planes, rows, nz), f32),
            pltpu.VMEM((planes, rows, nz), f32),
            pltpu.VMEM((planes, rows, nz), f32),
            pltpu.VMEM((slots, rows, nz), f32),
            pltpu.VMEM((slots, rows, nz), f32),
            pltpu.VMEM((slots, rows, nz), f32),
            pltpu.VMEM((planes, rows, nz), f32),
            pltpu.VMEM((planes, rows, nz), f32),
            pltpu.VMEM((2, group, rows, nz), f32),
            pltpu.VMEM((2, 2, HALO, rows, nz), f32),
            pltpu.VMEM((2, 2, 2, ngy, ly, nz), f32),
            pltpu.VMEM((3, group, 2, ngy, ly, nz), f32),
            pltpu.VMEM((3, count, lx, ly, nz), f32),
            pltpu.VMEM((count, 128), f32),
            pltpu.VMEM((count, count, 128), f32),
            pltpu.VMEM((count, 128), f32),
            pltpu.VMEM((groups, count, 128), f32),
            dma((3,)), dma((3, count)), dma((slots, ngy)), dma((3, count)), dma((slots, ngy)),
            dma((3, 2)), dma((3, 2)), dma((2, count)), dma((2, count)),
            dma((count,)), dma((count,)), dma((groups,)), dma((groups,)),
        ],
        compiler_params=pltpu.CompilerParams(
            collective_id=0, has_side_effects=True, vmem_limit_bytes=32 * 1024 * 1024),
        name="block_step",
    )(rhs, classes, supports)


def solution(mesh):
    ngx, ngy = mesh.shape["gx"], mesh.shape["gy"]
    spread_out = P(None, "gx", "gy", None)
    return jax.shard_map(
        functools.partial(local, ngx, ngy),
        mesh=mesh,
        in_specs=(spread_out, P("gx", "gy", None), P("gx", "gy", None)),
        out_specs=(spread_out, spread_out, spread_out),
        check_vma=False,
    )
```

time: 41.8 us -> 40.7 us (0.974)
  Pallas kernels: 36.8 us -> 35.7 us
    pallas_call x1, Pallas kernels: 36.8 us -> 35.7 us  [local(): pl.pallas_call(functools.partial(kernel, ngx, ngy), out_shape=[jax.ShapeD...]
where the time goes in v2:
time: 40.7 us; the launch traced here: 40.4 us
  Pallas kernels  35.7 us (88%)
  local copies, waits for them, and re-layouts  4.12 us (10%)
  between operations  0.65 us (2%)
    pallas_call x1, Pallas kernels, local(): pl.pallas_call(functools.partial(kernel, ngx, ngy), out_shape=[jax.ShapeD...  35.7 us
    unnamed x9, local copies, waits for them, and re-layouts  4.12 us

profile of v2, /device:TPU:0, one launch (start us, length us, event | category | flops | bytes accessed | tf_op | source)
XLA Modules:
  0.0 40.4 jit_solution(4643554940822274239)
XLA Ops:
  0.6 0.0 copy-start
  0.6 0.8 %copy-done = f32[8,2,8,128]{3,2,1,0:T(8,128)S(1)} copy-done((f32[8,2,8,128]{3,2,1,0:T(8,128)S(1)}, f32[8,2,8,128]{3,2,1,0:T(8,128)}, u32[]{:S(2)}) %copy-start) | copy-done | bytes 65560
  1.5 0.0 copy-start.1
  1.5 0.7 %copy-done.1 = s32[2,8,128]{2,1,0:T(8,128)S(1)} copy-done((s32[2,8,128]{2,1,0:T(8,128)S(1)}, s32[2,8,128]{2,1,0:T(8,128)}, u32[]{:S(2)}) %copy-start.1) | copy-done | bytes 8216
  2.2 0.0 copy-start.2
  2.2 0.7 %copy-done.2 = s32[2,8,128]{2,1,0:T(8,128)S(1)} copy-done((s32[2,8,128]{2,1,0:T(8,128)S(1)}, s32[2,8,128]{2,1,0:T(8,128)}, u32[]{:S(2)}) %copy-start.2) | copy-done | bytes 8216
  2.9 35.7 %block_step.1 = (f32[8,2,8,128]{3,2,1,0:T(8,128)S(1)}, f32[8,2,8,128]{3,2,1,0:T(8,128)S(1)}, f32[8,2,8,128]{3,2,1,0:T(8,128)S(1)}) custom-call(f32[8,2,8,128]{3,2,1,0:T(8,128)S(1)} %copy-done, s32[2,8,128]{2,1,0:T(8,128)S(1)} %copy-done.1, s32[2,8,128]{2,1,0:T(8,128)S(1)} %copy-done.2), custom_call_target="tpu_custom_call" | custom-call | tf_op jit(solution)/shard_map/block_step/pallas_call | solution.py:487
  38.5 0.6 %copy.9 = f32[8,2,8,128]{3,2,1,0:T(8,128)} copy(f32[8,2,8,128]{3,2,1,0:T(8,128)S(1)} %get-tuple-element.6) | data formatting | bytes 131072
  39.2 0.6 %copy.10 = f32[8,2,8,128]{3,2,1,0:T(8,128)} copy(f32[8,2,8,128]{3,2,1,0:T(8,128)S(1)} %get-tuple-element.7) | data formatting | bytes 131072
  39.8 0.6 %copy.11 = f32[8,2,8,128]{3,2,1,0:T(8,128)} copy(f32[8,2,8,128]{3,2,1,0:T(8,128)S(1)} %get-tuple-element.8) | data formatting | bytes 131072
Async XLA Ops:
  0.6 0.8 %copy-start = (f32[8,2,8,128]{3,2,1,0:T(8,128)S(1)}, f32[8,2,8,128]{3,2,1,0:T(8,128)}, u32[]{:S(2)}) copy-start(f32[8,2,8,128]{3,2,1,0:T(8,128)} %rhs_hbm.1) | copy-start | bytes 196612
  1.5 0.7 %copy-start.1 = (s32[2,8,128]{2,1,0:T(8,128)S(1)}, s32[2,8,128]{2,1,0:T(8,128)}, u32[]{:S(2)}) copy-start(s32[2,8,128]{2,1,0:T(8,128)} %classes_hbm.1) | copy-start | bytes 24580
  2.2 0.7 %copy-start.2 = (s32[2,8,128]{2,1,0:T(8,128)S(1)}, s32[2,8,128]{2,1,0:T(8,128)}, u32[]{:S(2)}) copy-start(s32[2,8,128]{2,1,0:T(8,128)} %supports_hbm.1) | copy-start | bytes 24580

commit v3 on v2

--- a/solution.py
+++ b/solution.py
@@ -12,6 +12,8 @@
 DAMP = 0.5
 HALO = 2
 
+DIRECT = 64
+
 MESH = pl.DeviceIdType.MESH
 EXACT = lax.Precision.HIGHEST
 
@@ -24,20 +26,15 @@
     return functools.cache(f)
 
 
-def halves(u):
-    top = u.astype(jnp.bfloat16)
-    return top, (u - top.astype(jnp.float32)).astype(jnp.bfloat16)
-
-
 def kernel(
     ngx, ngy,
-    rhs_hbm, classes_hbm, supports_hbm, sol_ref, res_ref, dir_ref,
-    rhs_ref, classes_ref, supports_ref,
-    mine, cext, rext, scales, weight, spring, cstep, rest, coarse, smooth, first,
+    rhs_hbm, classes_hbm, supports_hbm, sol_hbm, res_hbm, dir_hbm,
+    classes_ref, supports_ref, outs,
+    pack, ext, scales, weight, spring, cstep, rest, coarse, smooth, first,
     own_c, halo_c, halo_a, fields, returned, part, first_sums, group_sum, last_sums,
-    in_sem, gc_send, gc_recv, gr_send, gr_recv, x_send, x_recv, b_send, b_recv, a_send, a_recv, q_send, q_recv,
+    in_sem, out_sem, g_send, g_recv, x_send, x_recv, b_send, b_recv, a_send, a_recv, q_send, q_recv,
 ):
-    count, lx, ly, nz = rhs_ref.shape
+    count, lx, ly, nz = rhs_hbm.shape
     group = count // ngy
     groups = ngx // group
     slots = group + 2 * HALO
@@ -49,10 +46,16 @@
     others = [(me + o) % count for o in range(1, count)]
     other_groups = [(g + o) % groups for o in range(1, groups)]
 
+    devices = ngx * ngy
+    direct = devices <= DIRECT
+    place = gx * ngy + gy
+    team, seat = (devices, place) if direct else (count, me)
+    teammates = [(seat + o) % team for o in range(1, team)]
+
     loads = [
         pltpu.make_async_copy(classes_hbm, classes_ref, in_sem.at[0]),
         pltpu.make_async_copy(supports_hbm, supports_ref, in_sem.at[1]),
-        pltpu.make_async_copy(rhs_hbm, rhs_ref, in_sem.at[2]),
+        pltpu.make_async_copy(rhs_hbm, pack.at[:, 0], in_sem.at[2]),
     ]
     for load in loads:
         load.start()
@@ -70,19 +73,23 @@
             greet(member(at_group, j))
 
     has_below, has_above = g > 0, g < groups - 1
-    for j in others:
-        greet(member(g, j))
-    pl.when(has_below)(lambda: greet_group(g - 1))
-    pl.when(has_above)(lambda: greet_group(g + 1))
-    for q in range(groups):
-        pl.when(jnp.abs(q - g) > 1)(functools.partial(greet, (q * group + s, gy)))
-    below, above = has_below.astype(jnp.int32), has_above.astype(jnp.int32)
-    expected = (count - 1) + count * (below + above) + (groups - 1 - below - above)
+    if direct:
+        for t in teammates:
+            greet((t // ngy, t % ngy))
+        expected = devices - 1
+    else:
+        for j in others:
+            greet(member(g, j))
+        pl.when(has_below)(lambda: greet_group(g - 1))
+        pl.when(has_above)(lambda: greet_group(g + 1))
+        for q in range(groups):
+            pl.when(jnp.abs(q - g) > 1)(functools.partial(greet, (q * group + s, gy)))
+        below, above = has_below.astype(jnp.int32), has_above.astype(jnp.int32)
+        expected = (count - 1) + count * (below + above) + (groups - 1 - below - above)
 
     def clear(side):
         at = 0 if side == 0 else slots - HALO
-        cext[:, at : at + HALO] = jnp.zeros((2, HALO, 2, ngy, ly, nz), jnp.float32)
-        rext[at : at + HALO] = jnp.zeros((HALO, 2, ngy, ly, nz), jnp.float32)
+        ext[:, at : at + HALO] = jnp.zeros((3, HALO, 2, ngy, ly, nz), jnp.float32)
         for call in range(2):
             halo_c[call, side] = jnp.zeros((HALO, rows, nz), jnp.float32)
         halo_a[side] = jnp.zeros((2, 2, ngy, ly, nz), jnp.float32)
@@ -91,24 +98,20 @@
     pl.when(g == groups - 1)(lambda: clear(1))
     loads[0].wait()
     density = (classes_ref[...].astype(jnp.float32) + 1.0) / 4.0
-    mine[0] = 0.001 + density * density * density
+    stiff_own = 0.001 + density * density * density
     loads[1].wait()
-    mine[1] = supports_ref[...].astype(jnp.float32)
+    support_own = supports_ref[...].astype(jnp.float32)
+    for j in range(count):
+        pack[j, 1] = stiff_own
+        pack[j, 2] = support_own
     loads[2].wait()
     pl.semaphore_wait(barrier, expected)
 
-    def coef_copy(dg, j):
+    def gather_copy(dg, j):
         slot = s + HALO - dg * group
         return pltpu.make_async_remote_copy(
-            src_ref=mine, dst_ref=cext.at[:, slot, :, gy],
-            send_sem=gc_send.at[dg + 1, j], recv_sem=gc_recv.at[slot, gy],
-            device_id=member(g + dg, j), device_id_type=MESH)
-
-    def rhs_copy(dg, j):
-        slot = s + HALO - dg * group
-        return pltpu.make_async_remote_copy(
-            src_ref=rhs_ref.at[j], dst_ref=rext.at[slot, :, gy],
-            send_sem=gr_send.at[dg + 1, j], recv_sem=gr_recv.at[slot, gy],
+            src_ref=pack.at[j], dst_ref=ext.at[:, slot, :, gy],
+            send_sem=g_send.at[dg + 1, j], recv_sem=g_recv.at[slot, gy],
             device_id=member(g + dg, j), device_id_type=MESH)
 
     def outward(action):
@@ -117,37 +120,23 @@
 
             @pl.when(there & (slot >= 0) & (slot < slots))
             def _():
-                for make in (coef_copy, rhs_copy):
-                    for j in range(count):
-                        action(make(dg, j))
+                for j in range(count):
+                    action(gather_copy(dg, j))
 
     outward(lambda copy: copy.start())
-    for make in (coef_copy, rhs_copy):
-        for j in others:
-            make(0, j).start()
-    cext[:, s + HALO, :, gy] = mine[...]
-    rext[s + HALO, :, gy] = rhs_ref[me]
-
-    def wait_coef(slot, y):
+    for j in others:
+        gather_copy(0, j).start()
+    ext[:, s + HALO, :, gy] = pack[me]
+
+    def wait_slab(slot, y):
         pltpu.make_async_remote_copy(
-            src_ref=mine, dst_ref=cext.at[:, slot, :, y], send_sem=gc_send.at[0, 0],
-            recv_sem=gc_recv.at[slot, y], device_id=(gx, gy), device_id_type=MESH).wait_recv()
-
-    def wait_rhs(slot, y):
-        pltpu.make_async_remote_copy(
-            src_ref=rhs_ref.at[0], dst_ref=rext.at[slot, :, y], send_sem=gr_send.at[0, 0],
-            recv_sem=gr_recv.at[slot, y], device_id=(gx, gy), device_id_type=MESH).wait_recv()
-
-    def wait_all(wait):
-        def side(at):
-            for slot in range(at, at + HALO):
-                for y in range(ngy):
-                    wait(slot, y)
-
-        for j in others:
-            wait(HALO + j // ngy, j % ngy)
-        pl.when(has_below)(lambda: side(0))
-        pl.when(has_above)(lambda: side(HALO + group))
+            src_ref=pack.at[0], dst_ref=ext.at[:, slot, :, y], send_sem=g_send.at[0, 0],
+            recv_sem=g_recv.at[slot, y], device_id=(gx, gy), device_id_type=MESH).wait_recv()
+
+    def wait_side(at):
+        for slot in range(at, at + HALO):
+            for y in range(ngy):
+                wait_slab(slot, y)
 
     shape = (rows, nz)
     row_id, lane_id = axis_ids(shape, 0), axis_ids(shape, 1)
@@ -222,7 +211,10 @@
 
     lo, hi = 2 * HALO, planes - 2 * HALO
     near = range(HALO - 1, HALO + group + 1)
-    wait_all(wait_coef)
+    for j in others:
+        wait_slab(HALO + j // ngy, j % ngy)
+    pl.when(has_below)(lambda: wait_side(0))
+    pl.when(has_above)(lambda: wait_side(HALO + group))
 
     def inside(p):
         if p < lo:
@@ -236,7 +228,7 @@
         return amount / value if there is None else there * (amount / (value + (1.0 - there)))
 
     def stiff(p):
-        return cext[0, p // 2, p % 2].reshape(shape)
+        return ext[1, p // 2, p % 2].reshape(shape)
 
     diagonals = {}
     for p in range(lo - 3, hi + 4):
@@ -245,7 +237,7 @@
         scales[1, p] = e * (1.0 / 24.0)
         scales[2, p] = e * (1.0 / 48.0)
         if p < hi + 3:
-            tied = SPRING * cext[1, p // 2, p % 2].reshape(shape)
+            tied = SPRING * ext[2, p // 2, p % 2].reshape(shape)
             spring[p] = tied
             around = e + stiff(p + 1)
             around = around + after_y(around)
@@ -276,7 +268,7 @@
 
     pending = []
 
-    def correct(source, call):
+    def correct(source, call, meanwhile=lambda: None):
         def z(p):
             return source(p) * weight[p]
 
@@ -293,6 +285,7 @@
             own_c.at[call, pl.ds(0, HALO)], own_c.at[call, pl.ds(group - HALO, HALO)],
             halo_c.at[call, 0], halo_c.at[call, 1], call)
         pending.append(copies)
+        meanwhile()
         finish_edges(*copies)
 
         def swept(cell):
@@ -314,10 +307,8 @@
     def keep(f, p, u):
         fields[f, (p - lo) // 2, (p - lo) % 2] = u.reshape(ngy, ly, nz)
 
-    wait_all(wait_rhs)
-
     def given_plane(p):
-        return rext[p // 2, p % 2].reshape(shape)
+        return ext[0, p // 2, p % 2].reshape(shape)
 
     correct(given_plane, 0)
     for p, u in smoothed(given_plane, lo - 1, hi + 1):
@@ -361,10 +352,47 @@
             u = halo_a[1, (p - hi) // 2, (p - hi) % 2]
         return u.reshape(shape)
 
-    correct(product_plane, 1)
-    for p, u in smoothed(product_plane, lo, hi):
-        keep(2, p, u)
-    send_back(1, 2, 1)
+    def sum_copy(k, t):
+        to = (t // ngy, t % ngy) if direct else member(g, t)
+        return pltpu.make_async_remote_copy(
+            src_ref=part.at[k], dst_ref=first_sums.at[k, seat], send_sem=a_send.at[k, t],
+            recv_sem=a_recv.at[k, seat], device_id=to, device_id_type=MESH)
+
+    def sum_wait(k, t):
+        pltpu.make_async_remote_copy(
+            src_ref=part.at[k], dst_ref=first_sums.at[k, t], send_sem=a_send.at[k, t],
+            recv_sem=a_recv.at[k, t], device_id=(gx, gy), device_id_type=MESH).wait_recv()
+
+    def total_copy(k, q):
+        return pltpu.make_async_remote_copy(
+            src_ref=group_sum.at[k], dst_ref=last_sums.at[k, g], send_sem=q_send.at[k, q],
+            recv_sem=q_recv.at[k, g], device_id=(q * group + s, gy), device_id_type=MESH)
+
+    def total_wait(k, q):
+        pltpu.make_async_remote_copy(
+            src_ref=group_sum.at[k], dst_ref=last_sums.at[k, q], send_sem=q_send.at[k, q],
+            recv_sem=q_recv.at[k, q], device_id=(gx, gy), device_id_type=MESH).wait_recv()
+
+    def start_sum(k, value):
+        part[k] = jnp.zeros((count, 128), jnp.float32)
+        part[k, :, 0 : value.shape[1]] = value
+        for t in teammates:
+            sum_copy(k, t).start()
+        first_sums[k, seat] = part[k]
+
+    def finish_sum(k):
+        for t in teammates:
+            sum_wait(k, t)
+        total = jnp.sum(first_sums[k], axis=0)
+        if direct:
+            return total
+        group_sum[k] = total
+        for q in other_groups:
+            total_copy(k, q).start()
+        last_sums[k, g] = group_sum[k]
+        for q in other_groups:
+            total_wait(k, q)
+        return jnp.sum(last_sums[k], axis=0)
 
     def flat(block):
         parts = []
@@ -373,65 +401,32 @@
             parts += [turned[b] for b in range(ly)]
         return jnp.concatenate(parts, axis=1)
 
-    given = flat(rhs_ref[...])
-    for j in others:
-        wait_back(0, 0, 2, j)
-    field, product = flat(returned[0]), flat(returned[1])
-    for j in others:
-        wait_back(1, 2, 1, j)
-    twice = flat(returned[2])
-
     def dot(left, right, dims):
-        return lax.dot_general(left, right, (dims, ((), ())), preferred_element_type=jnp.float32)
-
-    left_top, left_low = halves(jnp.concatenate([field, product], axis=0))
-    right_top, right_low = halves(jnp.concatenate([product, given, field, twice], axis=0))
-    sums = dot(
-        jnp.concatenate([left_top, left_low, left_top], axis=1),
-        jnp.concatenate([right_top, right_top, right_low], axis=1), ((1,), (1,)))
-    wide = 4 * count
-    lane = axis_ids((count, wide), 1)
-    part[...] = jnp.zeros_like(part)
-    part[:, 0:wide] = jnp.where(lane < 2 * count, sums[:count], sums[count:])
-
-    def sum_copy(j):
-        return pltpu.make_async_remote_copy(
-            src_ref=part, dst_ref=first_sums.at[me], send_sem=a_send.at[j], recv_sem=a_recv.at[me],
-            device_id=member(g, j), device_id_type=MESH)
-
-    def sum_wait(j):
-        pltpu.make_async_remote_copy(
-            src_ref=part, dst_ref=first_sums.at[j], send_sem=a_send.at[j], recv_sem=a_recv.at[j],
-            device_id=(gx, gy), device_id_type=MESH).wait_recv()
-
-    for j in others:
-        sum_copy(j).start()
-    first_sums[me] = part[...]
-    for j in others:
-        sum_wait(j)
-    group_sum[...] = jnp.sum(first_sums[...], axis=0)
-
-    def total_copy(q):
-        return pltpu.make_async_remote_copy(
-            src_ref=group_sum, dst_ref=last_sums.at[g], send_sem=q_send.at[q], recv_sem=q_recv.at[g],
-            device_id=(q * group + s, gy), device_id_type=MESH)
-
-    def total_wait(q):
-        pltpu.make_async_remote_copy(
-            src_ref=group_sum, dst_ref=last_sums.at[q], send_sem=q_send.at[q], recv_sem=q_recv.at[q],
-            device_id=(gx, gy), device_id_type=MESH).wait_recv()
-
-    for q in other_groups:
-        total_copy(q).start()
-    last_sums[g] = group_sum[...]
-    for q in other_groups:
-        total_wait(q)
-    system = jnp.sum(last_sums[...], axis=0)
+        return lax.dot_general(
+            left, right, (dims, ((), ())), precision=EXACT, preferred_element_type=jnp.float32)
+
+    def first_products():
+        for j in others:
+            wait_back(0, 0, 2, j)
+        field, product, given = flat(returned[0]), flat(returned[1]), flat(pack[:, 0])
+        start_sum(0, dot(field, jnp.concatenate([product, given], axis=0), ((1,), (1,))))
+
+    correct(product_plane, 1, first_products)
+    for p, u in smoothed(product_plane, lo, hi):
+        keep(2, p, u)
+    send_back(1, 2, 1)
+
+    field, product, given = flat(returned[0]), flat(returned[1]), flat(pack[:, 0])
+    system = finish_sum(0)
 
     lane = axis_ids(system.shape, 1)
     row = axis_ids(system.shape, 0)
-    mirrored = pltpu.roll(system, system.shape[1] - 2 * count, 1)
-    system = jnp.where(lane < count, 0.5 * (system + mirrored), system)
+    crossed = jnp.transpose(system[:, 0:count])
+    square = 0.5 * (system[:, 0:count] + crossed)
+    same = axis_ids((count, count), 0) == axis_ids((count, count), 1)
+    unit = jnp.where(same, 1.0, 0.0)
+    rest_of = jnp.zeros((count, 128 - 4 * count), jnp.float32)
+    system = jnp.concatenate([square, system[:, count : 2 * count], crossed, unit, rest_of], axis=1)
     for k in range(count):
         column = jnp.sum(jnp.where(lane == k, system, 0.0), axis=1, keepdims=True)
         pivot_row = system[k : k + 1]
@@ -441,38 +436,53 @@
     def columns(n):
         return system[:, n * count : (n + 1) * count]
 
-    step = columns(1)
-    turn = jnp.dot(columns(3), step, precision=EXACT, preferred_element_type=jnp.float32) - columns(2)
+    step, turned_field, inverse_square = columns(1), columns(2), columns(3)
 
     def mixed(coef, u):
-        coef_top, u_top = [v.astype(jnp.bfloat16).astype(jnp.float32) for v in (coef, u)]
-        coefs = jnp.concatenate([coef_top, coef - coef_top, coef_top], axis=0).astype(jnp.bfloat16)
-        terms = jnp.concatenate([u_top, u_top, u - u_top], axis=0).astype(jnp.bfloat16)
-        return dot(coefs, terms, ((0,), (0,)))
-
-    def put(ref, u):
+        return dot(coef, u, ((0,), (0,)))
+
+    stores = []
+
+    def put(n, target, u):
         for a in range(lx):
             at = a * ly
             block = jnp.stack([u[:, (at + b) * nz : (at + b + 1) * nz] for b in range(ly)], axis=0)
-            ref[:, a] = jnp.swapaxes(block, 0, 1)
-
-    put(sol_ref, mixed(step, field))
-    put(res_ref, given - mixed(step, product))
-    put(dir_ref, field + mixed(jnp.concatenate([turn, -step], axis=0), jnp.concatenate([field, twice], axis=0)))
+            outs[n, :, a] = jnp.swapaxes(block, 0, 1)
+        stores.append(pltpu.make_async_copy(outs.at[n], target, out_sem.at[n]))
+        stores[-1].start()
+
+    put(0, sol_hbm, mixed(step, field))
+    put(1, res_hbm, given - mixed(step, product))
+
+    for j in others:
+        wait_back(1, 2, 1, j)
+    twice = flat(returned[2])
+    start_sum(1, dot(product, twice, ((1,), (1,))))
+    base = field - mixed(step, twice)
+    second = finish_sum(1)[:, 0:count]
+
+    def times(a, b):
+        return jnp.dot(a, b, precision=EXACT, preferred_element_type=jnp.float32)
+
+    turn = times(inverse_square, times(second, step)) - turned_field
+    put(2, dir_hbm, base + mixed(turn, field))
 
     outward(lambda copy: copy.wait_send())
-    for make in (coef_copy, rhs_copy):
-        for j in others:
-            make(0, j).wait_send()
+    for j in others:
+        gather_copy(0, j).wait_send()
     for copies in pending:
         drain_edges(*copies)
     for k, f, n in ((0, 0, 2), (1, 2, 1)):
         for j in others:
             back_copy(k, f, n, j).wait_send()
-    for j in others:
-        sum_copy(j).wait_send()
-    for q in other_groups:
-        total_copy(q).wait_send()
+    for k in range(2):
+        for t in teammates:
+            sum_copy(k, t).wait_send()
+        if not direct:
+            for q in other_groups:
+                total_copy(k, q).wait_send()
+    for store in stores:
+        store.wait()
 
 
 def local(ngx, ngy, rhs, classes, supports):
@@ -482,20 +492,20 @@
     slots = group + 2 * HALO
     rows = ngy * ly
     planes = 2 * slots
+    team = ngx * ngy if ngx * ngy <= DIRECT else count
     f32 = jnp.float32
     dma = pltpu.SemaphoreType.DMA
     return pl.pallas_call(
         functools.partial(kernel, ngx, ngy),
         out_shape=[jax.ShapeDtypeStruct(rhs.shape, f32)] * 3,
         in_specs=[pl.BlockSpec(memory_space=pltpu.HBM)] * 3,
-        out_specs=[pl.BlockSpec(memory_space=pltpu.VMEM)] * 3,
+        out_specs=[pl.BlockSpec(memory_space=pltpu.HBM)] * 3,
         scratch_shapes=[
-            pltpu.VMEM(rhs.shape, f32),
             pltpu.VMEM(classes.shape, jnp.int32),
             pltpu.VMEM(supports.shape, jnp.int32),
-            pltpu.VMEM((2, lx, ly, nz), f32),
-            pltpu.VMEM((2, slots, 2, ngy, ly, nz), f32),
-            pltpu.VMEM((slots, 2, ngy, ly, nz), f32),
+            pltpu.VMEM((3, count, lx, ly, nz), f32),
+            pltpu.VMEM((count, 3, lx, ly, nz), f32),
+            pltpu.VMEM((3, slots, 2, ngy, ly, nz), f32),
             pltpu.VMEM((3, planes, rows, nz), f32),
             pltpu.VMEM((planes, rows, nz), f32),
             pltpu.VMEM((planes, rows, nz), f32),
@@ -509,16 +519,16 @@
             pltpu.VMEM((2, 2, 2, ngy, ly, nz), f32),
             pltpu.VMEM((3, group, 2, ngy, ly, nz), f32),
             pltpu.VMEM((3, count, lx, ly, nz), f32),
-            pltpu.VMEM((count, 128), f32),
-            pltpu.VMEM((count, count, 128), f32),
-            pltpu.VMEM((count, 128), f32),
-            pltpu.VMEM((groups, count, 128), f32),
-            dma((3,)), dma((3, count)), dma((slots, ngy)), dma((3, count)), dma((slots, ngy)),
+            pltpu.VMEM((2, count, 128), f32),
+            pltpu.VMEM((2, team, count, 128), f32),
+            pltpu.VMEM((2, count, 128), f32),
+            pltpu.VMEM((2, groups, count, 128), f32),
+            dma((3,)), dma((3,)), dma((3, count)), dma((slots, ngy)),
             dma((3, 2)), dma((3, 2)), dma((2, count)), dma((2, count)),
-            dma((count,)), dma((count,)), dma((groups,)), dma((groups,)),
+            dma((2, team)), dma((2, team)), dma((2, groups)), dma((2, groups)),
         ],
         compiler_params=pltpu.CompilerParams(
-            collective_id=0, has_side_effects=True, vmem_limit_bytes=32 * 1024 * 1024),
+            collective_id=0, has_side_effects=True),
         name="block_step",
     )(rhs, classes, supports)
 

time: 40.7 us -> 41.5 us (1.020)
  Pallas kernels: 35.7 us -> 37.6 us
  local copies, waits for them, and re-layouts: 4.12 us -> 3 us
    pallas_call x1, Pallas kernels: 35.7 us -> 37.6 us  [local(): pl.pallas_call(functools.partial(kernel, ngx, ngy), out_shape=[jax.ShapeD...]
    unnamed x9 -> x7, local copies, waits for them, and re-layouts: 4.12 us -> 3 us
where the time goes in v3:
time: 41.5 us; the launch traced here: 41.3 us
  Pallas kernels  37.6 us (91%)
  local copies, waits for them, and re-layouts  3 us (7%)
  between operations  0.65 us (2%)
    pallas_call x1, Pallas kernels, local(): pl.pallas_call(functools.partial(kernel, ngx, ngy), out_shape=[jax.ShapeD...  37.6 us
    unnamed x7, local copies, waits for them, and re-layouts  3 us

profile of v3, /device:TPU:0, one launch (start us, length us, event | category | flops | bytes accessed | tf_op | source)
XLA Modules:
  0.0 41.3 jit_solution(7745828748780204602)
XLA Ops:
  0.6 37.6 %block_step.1 = (f32[8,2,8,128]{3,2,1,0:T(8,128)}, f32[8,2,8,128]{3,2,1,0:T(8,128)}, f32[8,2,8,128]{3,2,1,0:T(8,128)}) custom-call(f32[8,2,8,128]{3,2,1,0:T(8,128)} %rhs_hbm.1, s32[2,8,128]{2,1,0:T(8,128)} %classes_hbm.1, s32[2,8,128]{2,1,0:T(8,128)} %supports_hbm.1), custom_call_target="tpu_custom_call" | custom-call | tf_op jit(solution)/shard_map/block_step/pallas_call | solution.py:498
  38.3 0.0 copy-start.1
  38.3 1.5 %copy.9 = f32[8,2,8,128]{3,2,1,0:T(8,128)} copy(f32[8,2,8,128]{3,2,1,0:T(8,128)} %get-tuple-element.6) | data formatting | bytes 131072
  39.8 0.0 copy-done.1
  39.8 0.0 copy-start
  39.8 0.6 %copy.10 = f32[8,2,8,128]{3,2,1,0:T(8,128)} copy(f32[8,2,8,128]{3,2,1,0:T(8,128)S(1)} %copy-done.1) | data formatting | bytes 131072
  40.4 0.2 copy-done
  40.6 0.6 %copy.11 = f32[8,2,8,128]{3,2,1,0:T(8,128)} copy(f32[8,2,8,128]{3,2,1,0:T(8,128)S(1)} %copy-done) | data formatting | bytes 131072
Async XLA Ops:
  38.3 1.5 %copy-start.1 = (f32[8,2,8,128]{3,2,1,0:T(8,128)S(1)}, f32[8,2,8,128]{3,2,1,0:T(8,128)}, u32[]{:S(2)}) copy-start(f32[8,2,8,128]{3,2,1,0:T(8,128)} %get-tuple-element.7) | copy-start | bytes 196612
  39.8 0.9 %copy-start = (f32[8,2,8,128]{3,2,1,0:T(8,128)S(1)}, f32[8,2,8,128]{3,2,1,0:T(8,128)}, u32[]{:S(2)}) copy-start(f32[8,2,8,128]{3,2,1,0:T(8,128)} %get-tuple-element.8) | copy-start | bytes 196612

commit v4 on v3

--- a/solution.py
+++ b/solution.py
@@ -12,7 +12,7 @@
 DAMP = 0.5
 HALO = 2
 
-DIRECT = 64
+DIRECT = 0
 
 MESH = pl.DeviceIdType.MESH
 EXACT = lax.Precision.HIGHEST
@@ -30,7 +30,7 @@
     ngx, ngy,
     rhs_hbm, classes_hbm, supports_hbm, sol_hbm, res_hbm, dir_hbm,
     classes_ref, supports_ref, outs,
-    pack, ext, scales, weight, spring, cstep, rest, coarse, smooth, first,
+    flats, pack, ext, scales, weight, spring, cstep, rest, coarse, smooth, first,
     own_c, halo_c, halo_a, fields, returned, part, first_sums, group_sum, last_sums,
     in_sem, out_sem, g_send, g_recv, x_send, x_recv, b_send, b_recv, a_send, a_recv, q_send, q_recv,
 ):
@@ -380,16 +380,19 @@
             sum_copy(k, t).start()
         first_sums[k, seat] = part[k]
 
-    def finish_sum(k):
+    def carry_sum(k):
         for t in teammates:
             sum_wait(k, t)
-        total = jnp.sum(first_sums[k], axis=0)
+        group_sum[k] = jnp.sum(first_sums[k], axis=0)
         if direct:
-            return total
-        group_sum[k] = total
+            return
         for q in other_groups:
             total_copy(k, q).start()
         last_sums[k, g] = group_sum[k]
+
+    def finish_sum(k):
+        if direct:
+            return group_sum[k]
         for q in other_groups:
             total_wait(k, q)
         return jnp.sum(last_sums[k], axis=0)
@@ -409,14 +412,16 @@
         for j in others:
             wait_back(0, 0, 2, j)
         field, product, given = flat(returned[0]), flat(returned[1]), flat(pack[:, 0])
+        flats[0], flats[1], flats[2] = field, product, given
         start_sum(0, dot(field, jnp.concatenate([product, given], axis=0), ((1,), (1,))))
 
     correct(product_plane, 1, first_products)
+    carry_sum(0)
     for p, u in smoothed(product_plane, lo, hi):
         keep(2, p, u)
     send_back(1, 2, 1)
 
-    field, product, given = flat(returned[0]), flat(returned[1]), flat(pack[:, 0])
+    field, product, given = flats[0], flats[1], flats[2]
     system = finish_sum(0)
 
     lane = axis_ids(system.shape, 1)
@@ -459,6 +464,7 @@
     twice = flat(returned[2])
     start_sum(1, dot(product, twice, ((1,), (1,))))
     base = field - mixed(step, twice)
+    carry_sum(1)
     second = finish_sum(1)[:, 0:count]
 
     def times(a, b):
@@ -485,6 +491,15 @@
         store.wait()
 
 
+def hand_over(sol_in, res_in, dir_in, sol_out, res_out, dir_out, sems):
+    pairs = ((sol_in, sol_out), (res_in, res_out), (dir_in, dir_out))
+    copies = [pltpu.make_async_copy(source, target, sems.at[n]) for n, (source, target) in enumerate(pairs)]
+    for copy in copies:
+        copy.start()
+    for copy in copies:
+        copy.wait()
+
+
 def local(ngx, ngy, rhs, classes, supports):
     count, lx, ly, nz = rhs.shape
     group = count // ngy
@@ -495,7 +510,7 @@
     team = ngx * ngy if ngx * ngy <= DIRECT else count
     f32 = jnp.float32
     dma = pltpu.SemaphoreType.DMA
-    return pl.pallas_call(
+    results = pl.pallas_call(
         functools.partial(kernel, ngx, ngy),
         out_shape=[jax.ShapeDtypeStruct(rhs.shape, f32)] * 3,
         in_specs=[pl.BlockSpec(memory_space=pltpu.HBM)] * 3,
@@ -504,6 +519,7 @@
             pltpu.VMEM(classes.shape, jnp.int32),
             pltpu.VMEM(supports.shape, jnp.int32),
             pltpu.VMEM((3, count, lx, ly, nz), f32),
+            pltpu.VMEM((3, count, lx * ly * nz), f32),
             pltpu.VMEM((count, 3, lx, ly, nz), f32),
             pltpu.VMEM((3, slots, 2, ngy, ly, nz), f32),
             pltpu.VMEM((3, planes, rows, nz), f32),
@@ -531,6 +547,14 @@
             collective_id=0, has_side_effects=True),
         name="block_step",
     )(rhs, classes, supports)
+    return pl.pallas_call(
+        hand_over,
+        out_shape=[jax.ShapeDtypeStruct(rhs.shape, f32)] * 3,
+        in_specs=[pl.BlockSpec(memory_space=pltpu.HBM)] * 3,
+        out_specs=[pl.BlockSpec(memory_space=pltpu.HBM)] * 3,
+        scratch_shapes=[dma((3,))],
+        name="hand_over",
+    )(*results)
 
 
 def solution(mesh):

time: 41.5 us -> 46.4 us (1.12)
  Pallas kernels: 37.6 us -> 45.6 us
  local copies, waits for them, and re-layouts: 3 us -> 0 us
    pallas_call x0 -> x1, Pallas kernels: none -> 7.09 us  [local(): pl.pallas_call(hand_over, out_shape=[jax.ShapeDtypeStruct(rhs.shape, f32)...]
    unnamed x7 -> x0, local copies, waits for them, and re-layouts: 3 us -> none
    pallas_call x1, Pallas kernels: 37.6 us -> 38.5 us  [local(): pl.pallas_call(functools.partial(kernel, ngx, ngy), out_shape=[jax.ShapeD...]
where the time goes in v4:
time: 46.4 us; the launch traced here: 46.2 us
  Pallas kernels  45.6 us (98%)
  between operations  0.64 us (1%)
    pallas_call x1, Pallas kernels, local(): pl.pallas_call(functools.partial(kernel, ngx, ngy), out_shape=[jax.ShapeD...  38.5 us
    pallas_call x1, Pallas kernels, local(): pl.pallas_call(hand_over, out_shape=[jax.ShapeDtypeStruct(rhs.shape, f32)...  7.09 us

profile of v4, /device:TPU:0, one launch (start us, length us, event | category | flops | bytes accessed | tf_op | source)
XLA Modules:
  0.0 46.2 jit_solution(5930694442135819047)
XLA Ops:
  0.6 38.5 %block_step.1 = (f32[8,2,8,128]{3,2,1,0:T(8,128)}, f32[8,2,8,128]{3,2,1,0:T(8,128)}, f32[8,2,8,128]{3,2,1,0:T(8,128)}) custom-call(f32[8,2,8,128]{3,2,1,0:T(8,128)} %rhs_hbm.1, s32[2,8,128]{2,1,0:T(8,128)} %classes_hbm.1, s32[2,8,128]{2,1,0:T(8,128)} %supports_hbm.1), custom_call_target="tpu_custom_call" | custom-call | tf_op jit(solution)/shard_map/block_step/pallas_call | solution.py:513
  39.1 7.1 %hand_over.1 = (f32[8,2,8,128]{3,2,1,0:T(8,128)}, f32[8,2,8,128]{3,2,1,0:T(8,128)}, f32[8,2,8,128]{3,2,1,0:T(8,128)}) custom-call(f32[8,2,8,128]{3,2,1,0:T(8,128)} %get-tuple-element.6.sol_in, f32[8,2,8,128]{3,2,1,0:T(8,128)} %get-tuple-element.7.res_in, f32[8,2,8,128]{3,2,1,0:T(8,128)} %get-tuple-element.8.dir_in), custom_call_target="tpu_custom_call" | custom-call | tf_op jit(solution)/shard_map/hand_over/pallas_call | solution.py:550

commit v5 on v4

--- a/solution.py
+++ b/solution.py
@@ -28,13 +28,12 @@
 
 def kernel(
     ngx, ngy,
-    rhs_hbm, classes_hbm, supports_hbm, sol_hbm, res_hbm, dir_hbm,
-    classes_ref, supports_ref, outs,
+    rhs_ref, coef_ref, sol_ref, res_ref, dir_ref,
     flats, pack, ext, scales, weight, spring, cstep, rest, coarse, smooth, first,
     own_c, halo_c, halo_a, fields, returned, part, first_sums, group_sum, last_sums,
-    in_sem, out_sem, g_send, g_recv, x_send, x_recv, b_send, b_recv, a_send, a_recv, q_send, q_recv,
+    g_send, g_recv, x_send, x_recv, b_send, b_recv, a_send, a_recv, q_send, q_recv,
 ):
-    count, lx, ly, nz = rhs_hbm.shape
+    count, lx, ly, nz = rhs_ref.shape
     group = count // ngy
     groups = ngx // group
     slots = group + 2 * HALO
@@ -43,22 +42,20 @@
     gx, gy = lax.axis_index("gx"), lax.axis_index("gy")
     g, s = gx // group, gx % group
     me = s * ngy + gy
-    others = [(me + o) % count for o in range(1, count)]
-    other_groups = [(g + o) % groups for o in range(1, groups)]
+
+    def each(size, at, action):
+        @pl.loop(1, size)
+        def _(o):
+            action((at + o) % size)
+
+    others = functools.partial(each, count, me)
+    other_groups = functools.partial(each, groups, g)
 
     devices = ngx * ngy
     direct = devices <= DIRECT
     place = gx * ngy + gy
     team, seat = (devices, place) if direct else (count, me)
-    teammates = [(seat + o) % team for o in range(1, team)]
-
-    loads = [
-        pltpu.make_async_copy(classes_hbm, classes_ref, in_sem.at[0]),
-        pltpu.make_async_copy(supports_hbm, supports_ref, in_sem.at[1]),
-        pltpu.make_async_copy(rhs_hbm, pack.at[:, 0], in_sem.at[2]),
-    ]
-    for load in loads:
-        load.start()
+    teammates = functools.partial(each, team, seat)
 
     def member(at_group, j):
         return (at_group * group + j // ngy, j % ngy)
@@ -69,17 +66,16 @@
         pl.semaphore_signal(barrier, inc=1, device_id=target, device_id_type=MESH)
 
     def greet_group(at_group):
-        for j in range(count):
+        @pl.loop(0, count)
+        def _(j):
             greet(member(at_group, j))
 
     has_below, has_above = g > 0, g < groups - 1
     if direct:
-        for t in teammates:
-            greet((t // ngy, t % ngy))
+        teammates(lambda t: greet((t // ngy, t % ngy)))
         expected = devices - 1
     else:
-        for j in others:
-            greet(member(g, j))
+        others(lambda j: greet(member(g, j)))
         pl.when(has_below)(lambda: greet_group(g - 1))
         pl.when(has_above)(lambda: greet_group(g + 1))
         for q in range(groups):
@@ -96,15 +92,9 @@
 
     pl.when(g == 0)(lambda: clear(0))
     pl.when(g == groups - 1)(lambda: clear(1))
-    loads[0].wait()
-    density = (classes_ref[...].astype(jnp.float32) + 1.0) / 4.0
-    stiff_own = 0.001 + density * density * density
-    loads[1].wait()
-    support_own = supports_ref[...].astype(jnp.float32)
+    pack[:, 0] = rhs_ref[...]
     for j in range(count):
-        pack[j, 1] = stiff_own
-        pack[j, 2] = support_own
-    loads[2].wait()
+        pack[j, 1:3] = coef_ref[...]
     pl.semaphore_wait(barrier, expected)
 
     def gather_copy(dg, j):
@@ -120,12 +110,12 @@
 
             @pl.when(there & (slot >= 0) & (slot < slots))
             def _():
-                for j in range(count):
+                @pl.loop(0, count)
+                def _(j):
                     action(gather_copy(dg, j))
 
     outward(lambda copy: copy.start())
-    for j in others:
-        gather_copy(0, j).start()
+    others(lambda j: gather_copy(0, j).start())
     ext[:, s + HALO, :, gy] = pack[me]
 
     def wait_slab(slot, y):
@@ -134,9 +124,9 @@
             recv_sem=g_recv.at[slot, y], device_id=(gx, gy), device_id_type=MESH).wait_recv()
 
     def wait_side(at):
-        for slot in range(at, at + HALO):
-            for y in range(ngy):
-                wait_slab(slot, y)
+        @pl.loop(0, HALO * ngy)
+        def _(i):
+            wait_slab(at + i // ngy, i % ngy)
 
     shape = (rows, nz)
     row_id, lane_id = axis_ids(shape, 0), axis_ids(shape, 1)
@@ -211,8 +201,7 @@
 
     lo, hi = 2 * HALO, planes - 2 * HALO
     near = range(HALO - 1, HALO + group + 1)
-    for j in others:
-        wait_slab(HALO + j // ngy, j % ngy)
+    others(lambda j: wait_slab(HALO + j // ngy, j % ngy))
     pl.when(has_below)(lambda: wait_side(0))
     pl.when(has_above)(lambda: wait_side(HALO + group))
 
@@ -335,8 +324,7 @@
             device_id=(gx, gy), device_id_type=MESH).wait_recv()
 
     def send_back(k, f, n):
-        for j in others:
-            back_copy(k, f, n, j).start()
+        others(lambda j: back_copy(k, f, n, j).start())
         for i in range(f, f + n):
             returned[i, me] = fields[i, s, :, gy]
 
@@ -376,25 +364,21 @@
     def start_sum(k, value):
         part[k] = jnp.zeros((count, 128), jnp.float32)
         part[k, :, 0 : value.shape[1]] = value
-        for t in teammates:
-            sum_copy(k, t).start()
+        teammates(lambda t: sum_copy(k, t).start())
         first_sums[k, seat] = part[k]
 
     def carry_sum(k):
-        for t in teammates:
-            sum_wait(k, t)
+        teammates(lambda t: sum_wait(k, t))
         group_sum[k] = jnp.sum(first_sums[k], axis=0)
         if direct:
             return
-        for q in other_groups:
-            total_copy(k, q).start()
+        other_groups(lambda q: total_copy(k, q).start())
         last_sums[k, g] = group_sum[k]
 
     def finish_sum(k):
         if direct:
             return group_sum[k]
-        for q in other_groups:
-            total_wait(k, q)
+        other_groups(lambda q: total_wait(k, q))
         return jnp.sum(last_sums[k], axis=0)
 
     def flat(block):
@@ -409,8 +393,7 @@
             left, right, (dims, ((), ())), precision=EXACT, preferred_element_type=jnp.float32)
 
     def first_products():
-        for j in others:
-            wait_back(0, 0, 2, j)
+        others(lambda j: wait_back(0, 0, 2, j))
         field, product, given = flat(returned[0]), flat(returned[1]), flat(pack[:, 0])
         flats[0], flats[1], flats[2] = field, product, given
         start_sum(0, dot(field, jnp.concatenate([product, given], axis=0), ((1,), (1,))))
@@ -446,21 +429,16 @@
     def mixed(coef, u):
         return dot(coef, u, ((0,), (0,)))
 
-    stores = []
-
-    def put(n, target, u):
+    def put(target, u):
         for a in range(lx):
             at = a * ly
             block = jnp.stack([u[:, (at + b) * nz : (at + b + 1) * nz] for b in range(ly)], axis=0)
-            outs[n, :, a] = jnp.swapaxes(block, 0, 1)
-        stores.append(pltpu.make_async_copy(outs.at[n], target, out_sem.at[n]))
-        stores[-1].start()
-
-    put(0, sol_hbm, mixed(step, field))
-    put(1, res_hbm, given - mixed(step, product))
-
-    for j in others:
-        wait_back(1, 2, 1, j)
+            target[:, a] = jnp.swapaxes(block, 0, 1)
+
+    put(sol_ref, mixed(step, field))
+    put(res_ref, given - mixed(step, product))
+
+    others(lambda j: wait_back(1, 2, 1, j))
     twice = flat(returned[2])
     start_sum(1, dot(product, twice, ((1,), (1,))))
     base = field - mixed(step, twice)
@@ -471,24 +449,18 @@
         return jnp.dot(a, b, precision=EXACT, preferred_element_type=jnp.float32)
 
     turn = times(inverse_square, times(second, step)) - turned_field
-    put(2, dir_hbm, base + mixed(turn, field))
+    put(dir_ref, base + mixed(turn, field))
 
     outward(lambda copy: copy.wait_send())
-    for j in others:
-        gather_copy(0, j).wait_send()
+    others(lambda j: gather_copy(0, j).wait_send())
     for copies in pending:
         drain_edges(*copies)
     for k, f, n in ((0, 0, 2), (1, 2, 1)):
-        for j in others:
-            back_copy(k, f, n, j).wait_send()
+        others(lambda j: back_copy(k, f, n, j).wait_send())
     for k in range(2):
-        for t in teammates:
-            sum_copy(k, t).wait_send()
+        teammates(lambda t: sum_copy(k, t).wait_send())
         if not direct:
-            for q in other_groups:
-                total_copy(k, q).wait_send()
-    for store in stores:
-        store.wait()
+            other_groups(lambda q: total_copy(k, q).wait_send())
 
 
 def hand_over(sol_in, res_in, dir_in, sol_out, res_out, dir_out, sems):
@@ -510,15 +482,14 @@
     team = ngx * ngy if ngx * ngy <= DIRECT else count
     f32 = jnp.float32
     dma = pltpu.SemaphoreType.DMA
+    density = (classes.astype(f32) + 1.0) / 4.0
+    coef = jnp.stack([0.001 + density * density * density, supports.astype(f32)])
     results = pl.pallas_call(
         functools.partial(kernel, ngx, ngy),
         out_shape=[jax.ShapeDtypeStruct(rhs.shape, f32)] * 3,
-        in_specs=[pl.BlockSpec(memory_space=pltpu.HBM)] * 3,
-        out_specs=[pl.BlockSpec(memory_space=pltpu.HBM)] * 3,
+        in_specs=[pl.BlockSpec(memory_space=pltpu.VMEM)] * 2,
+        out_specs=[pl.BlockSpec(memory_space=pltpu.VMEM)] * 3,
         scratch_shapes=[
-            pltpu.VMEM(classes.shape, jnp.int32),
-            pltpu.VMEM(supports.shape, jnp.int32),
-            pltpu.VMEM((3, count, lx, ly, nz), f32),
             pltpu.VMEM((3, count, lx * ly * nz), f32),
             pltpu.VMEM((count, 3, lx, ly, nz), f32),
             pltpu.VMEM((3, slots, 2, ngy, ly, nz), f32),
@@ -539,19 +510,20 @@
             pltpu.VMEM((2, team, count, 128), f32),
             pltpu.VMEM((2, count, 128), f32),
             pltpu.VMEM((2, groups, count, 128), f32),
-            dma((3,)), dma((3,)), dma((3, count)), dma((slots, ngy)),
+            dma((3, count)), dma((slots, ngy)),
             dma((3, 2)), dma((3, 2)), dma((2, count)), dma((2, count)),
             dma((2, team)), dma((2, team)), dma((2, groups)), dma((2, groups)),
         ],
         compiler_params=pltpu.CompilerParams(
-            collective_id=0, has_side_effects=True),
+            collective_id=0, has_side_effects=True, vmem_limit_bytes=32 * 1024 * 1024),
         name="block_step",
-    )(rhs, classes, supports)
+    )(rhs, coef)
     return pl.pallas_call(
         hand_over,
         out_shape=[jax.ShapeDtypeStruct(rhs.shape, f32)] * 3,
-        in_specs=[pl.BlockSpec(memory_space=pltpu.HBM)] * 3,
+        in_specs=[pl.BlockSpec(memory_space=pltpu.VMEM)] * 3,
         out_specs=[pl.BlockSpec(memory_space=pltpu.HBM)] * 3,
+        compiler_params=pltpu.CompilerParams(vmem_limit_bytes=4 * 1024 * 1024),
         scratch_shapes=[dma((3,))],
         name="hand_over",
     )(*results)

time: 46.4 us -> 41.3 us (0.89)
  Pallas kernels: 45.6 us -> 38.9 us
  other arithmetic: 0 us -> 1.44 us
    pallas_call x1, Pallas kernels: 7.09 us -> 0.7 us  [local(): pl.pallas_call(hand_over, out_shape=[jax.ShapeDtypeStruct(rhs.shape, f32)...]
    another operation x0 -> x3, other arithmetic: none -> 1.44 us  [local(): jnp.stack([0.001 + density * density * density, supports.astype(f32)])]
where the time goes in v5:
time: 41.3 us; the launch traced here: 41 us
  Pallas kernels  38.9 us (94%)
  other arithmetic  1.44 us (3%)
  between operations  0.65 us (2%)
    pallas_call x1, Pallas kernels, local(): pl.pallas_call(functools.partial(kernel, ngx, ngy), out_shape=[jax.ShapeD...  38.2 us
    another operation x3, other arithmetic, local(): jnp.stack([0.001 + density * density * density, supports.astype(f32)])  1.44 us

profile of v5, /device:TPU:0, one launch (start us, length us, event | category | flops | bytes accessed | tf_op | source)
XLA Modules:
  0.0 41.0 jit_solution(5371530133127752274)
XLA Ops:
  0.6 0.0 copy-start
  0.6 0.7 %fusion.1 = f32[1,2,8,128]{3,2,1,0:T(8,128)S(1)} fusion(s32[2,8,128]{2,1,0:T(8,128)} %param.4), kind=kLoop, calls=%fused_computation.3 | loop fusion | flops 12288 | bytes 16384 | tf_op jit(solution)/shard_map/stack | solution.py:486
  1.4 0.7 %convert_bitcast_fusion = f32[1,2,8,128]{3,2,1,0:T(8,128)S(1)} fusion(s32[2,8,128]{2,1,0:T(8,128)} %param.5), kind=kLoop, calls=%fused_computation.4 | loop fusion | flops 2048 | bytes 16384 | tf_op jit(solution)/shard_map/stack | solution.py:486
  2.1 0.0 copy-done
  2.1 38.2 %block_step.1 = (f32[8,2,8,128]{3,2,1,0:T(8,128)S(1)}, f32[8,2,8,128]{3,2,1,0:T(8,128)S(1)}, f32[8,2,8,128]{3,2,1,0:T(8,128)S(1)}) custom-call(f32[8,2,8,128]{3,2,1,0:T(8,128)S(1)} %copy-done, f32[2,2,8,128]{3,2,1,0:T(8,128)S(1)} %pad_maximum_fusion.coef_ref), custom_call_target="tpu_custom_call" | custom-call | tf_op jit(solution)/shard_map/block_step/pallas_call | solution.py:487
  40.3 0.7 %hand_over.1 = (f32[8,2,8,128]{3,2,1,0:T(8,128)}, f32[8,2,8,128]{3,2,1,0:T(8,128)}, f32[8,2,8,128]{3,2,1,0:T(8,128)}) custom-call(f32[8,2,8,128]{3,2,1,0:T(8,128)S(1)} %get-tuple-element.6.sol_in, f32[8,2,8,128]{3,2,1,0:T(8,128)S(1)} %get-tuple-element.7.res_in, f32[8,2,8,128]{3,2,1,0:T(8,128)S(1)} %get-tuple-element.8.dir_in), custom_call_target="tpu_custom_call" | custom-call | tf_op jit(solution)/shard_map/hand_over/pallas_call | solution.py:521
  (1 shorter events, 0.0 us)
Async XLA Ops:
  0.6 1.5 %copy-start = (f32[8,2,8,128]{3,2,1,0:T(8,128)S(1)}, f32[8,2,8,128]{3,2,1,0:T(8,128)}, u32[]{:S(2)}) copy-start(f32[8,2,8,128]{3,2,1,0:T(8,128)} %rhs_ref.1) | copy-start | bytes 196612

commit v6 on v2

--- a/solution.py
+++ b/solution.py
@@ -31,11 +31,10 @@
 
 def kernel(
     ngx, ngy,
-    rhs_hbm, classes_hbm, supports_hbm, sol_ref, res_ref, dir_ref,
-    rhs_ref, classes_ref, supports_ref,
-    mine, cext, rext, scales, weight, spring, cstep, rest, coarse, smooth, first,
+    rhs_ref, mine, sol_ref, res_ref, dir_ref,
+    cext, rext, scales, weight, spring, cstep, rest, coarse, smooth, first,
     own_c, halo_c, halo_a, fields, returned, part, first_sums, group_sum, last_sums,
-    in_sem, gc_send, gc_recv, gr_send, gr_recv, x_send, x_recv, b_send, b_recv, a_send, a_recv, q_send, q_recv,
+    gc_send, gc_recv, gr_send, gr_recv, x_send, x_recv, b_send, b_recv, a_send, a_recv, q_send, q_recv,
 ):
     count, lx, ly, nz = rhs_ref.shape
     group = count // ngy
@@ -49,14 +48,6 @@
     others = [(me + o) % count for o in range(1, count)]
     other_groups = [(g + o) % groups for o in range(1, groups)]
 
-    loads = [
-        pltpu.make_async_copy(classes_hbm, classes_ref, in_sem.at[0]),
-        pltpu.make_async_copy(supports_hbm, supports_ref, in_sem.at[1]),
-        pltpu.make_async_copy(rhs_hbm, rhs_ref, in_sem.at[2]),
-    ]
-    for load in loads:
-        load.start()
-
     def member(at_group, j):
         return (at_group * group + j // ngy, j % ngy)
 
@@ -89,12 +80,6 @@
 
     pl.when(g == 0)(lambda: clear(0))
     pl.when(g == groups - 1)(lambda: clear(1))
-    loads[0].wait()
-    density = (classes_ref[...].astype(jnp.float32) + 1.0) / 4.0
-    mine[0] = 0.001 + density * density * density
-    loads[1].wait()
-    mine[1] = supports_ref[...].astype(jnp.float32)
-    loads[2].wait()
     pl.semaphore_wait(barrier, expected)
 
     def coef_copy(dg, j):
@@ -475,6 +460,15 @@
         total_copy(q).wait_send()
 
 
+def hand_over(sol_in, res_in, dir_in, sol_out, res_out, dir_out, sems):
+    pairs = ((sol_in, sol_out), (res_in, res_out), (dir_in, dir_out))
+    copies = [pltpu.make_async_copy(source, target, sems.at[n]) for n, (source, target) in enumerate(pairs)]
+    for copy in copies:
+        copy.start()
+    for copy in copies:
+        copy.wait()
+
+
 def local(ngx, ngy, rhs, classes, supports):
     count, lx, ly, nz = rhs.shape
     group = count // ngy
@@ -484,16 +478,14 @@
     planes = 2 * slots
     f32 = jnp.float32
     dma = pltpu.SemaphoreType.DMA
-    return pl.pallas_call(
+    density = (classes.astype(f32) + 1.0) / 4.0
+    coef = jnp.stack([0.001 + density * density * density, supports.astype(f32)])
+    results = pl.pallas_call(
         functools.partial(kernel, ngx, ngy),
         out_shape=[jax.ShapeDtypeStruct(rhs.shape, f32)] * 3,
-        in_specs=[pl.BlockSpec(memory_space=pltpu.HBM)] * 3,
+        in_specs=[pl.BlockSpec(memory_space=pltpu.VMEM)] * 2,
         out_specs=[pl.BlockSpec(memory_space=pltpu.VMEM)] * 3,
         scratch_shapes=[
-            pltpu.VMEM(rhs.shape, f32),
-            pltpu.VMEM(classes.shape, jnp.int32),
-            pltpu.VMEM(supports.shape, jnp.int32),
-            pltpu.VMEM((2, lx, ly, nz), f32),
             pltpu.VMEM((2, slots, 2, ngy, ly, nz), f32),
             pltpu.VMEM((slots, 2, ngy, ly, nz), f32),
             pltpu.VMEM((3, planes, rows, nz), f32),
@@ -513,14 +505,23 @@
             pltpu.VMEM((count, count, 128), f32),
             pltpu.VMEM((count, 128), f32),
             pltpu.VMEM((groups, count, 128), f32),
-            dma((3,)), dma((3, count)), dma((slots, ngy)), dma((3, count)), dma((slots, ngy)),
+            dma((3, count)), dma((slots, ngy)), dma((3, count)), dma((slots, ngy)),
             dma((3, 2)), dma((3, 2)), dma((2, count)), dma((2, count)),
             dma((count,)), dma((count,)), dma((groups,)), dma((groups,)),
         ],
         compiler_params=pltpu.CompilerParams(
             collective_id=0, has_side_effects=True, vmem_limit_bytes=32 * 1024 * 1024),
         name="block_step",
-    )(rhs, classes, supports)
+    )(rhs, coef)
+    return pl.pallas_call(
+        hand_over,
+        out_shape=[jax.ShapeDtypeStruct(rhs.shape, f32)] * 3,
+        in_specs=[pl.BlockSpec(memory_space=pltpu.VMEM)] * 3,
+        out_specs=[pl.BlockSpec(memory_space=pltpu.HBM)] * 3,
+        compiler_params=pltpu.CompilerParams(vmem_limit_bytes=4 * 1024 * 1024),
+        scratch_shapes=[dma((3,))],
+        name="hand_over",
+    )(*results)
 
 
 def solution(mesh):

time: 40.7 us -> 38.6 us (0.948)
  local copies, waits for them, and re-layouts: 4.12 us -> 0.01 us
  other arithmetic: 0 us -> 1.44 us
  Pallas kernels: 35.7 us -> 36.2 us
    unnamed x9 -> x2, local copies, waits for them, and re-layouts: 4.12 us -> 0.01 us
    another operation x0 -> x3, other arithmetic: none -> 1.44 us  [local(): jnp.stack([0.001 + density * density * density, supports.astype(f32)])]
    pallas_call x0 -> x1, Pallas kernels: none -> 0.7 us  [local(): pl.pallas_call(hand_over, out_shape=[jax.ShapeDtypeStruct(rhs.shape, f32)...]
where the time goes in v6:
time: 38.6 us; the launch traced here: 38.3 us
  Pallas kernels  36.2 us (94%)
  other arithmetic  1.44 us (4%)
  between operations  0.65 us (2%)
    pallas_call x1, Pallas kernels, local(): pl.pallas_call(functools.partial(kernel, ngx, ngy), out_shape=[jax.ShapeD...  35.5 us
    another operation x3, other arithmetic, local(): jnp.stack([0.001 + density * density * density, supports.astype(f32)])  1.44 us

profile of v6, /device:TPU:0, one launch (start us, length us, event | category | flops | bytes accessed | tf_op | source)
XLA Modules:
  0.0 38.3 jit_solution(4145469707340420300)
XLA Ops:
  0.6 0.0 copy-start
  0.6 0.7 %fusion.1 = f32[1,2,8,128]{3,2,1,0:T(8,128)S(1)} fusion(s32[2,8,128]{2,1,0:T(8,128)} %param.4), kind=kLoop, calls=%fused_computation.3 | loop fusion | flops 12288 | bytes 16384 | tf_op jit(solution)/shard_map/stack | solution.py:482
  1.4 0.7 %convert_bitcast_fusion = f32[1,2,8,128]{3,2,1,0:T(8,128)S(1)} fusion(s32[2,8,128]{2,1,0:T(8,128)} %param.5), kind=kLoop, calls=%fused_computation.4 | loop fusion | flops 2048 | bytes 16384 | tf_op jit(solution)/shard_map/stack | solution.py:482
  2.1 0.0 copy-done
  2.1 35.5 %block_step.1 = (f32[8,2,8,128]{3,2,1,0:T(8,128)S(1)}, f32[8,2,8,128]{3,2,1,0:T(8,128)S(1)}, f32[8,2,8,128]{3,2,1,0:T(8,128)S(1)}) custom-call(f32[8,2,8,128]{3,2,1,0:T(8,128)S(1)} %copy-done, f32[2,2,8,128]{3,2,1,0:T(8,128)S(1)} %pad_maximum_fusion.mine), custom_call_target="tpu_custom_call" | custom-call | tf_op jit(solution)/shard_map/block_step/pallas_call | solution.py:483
  37.6 0.7 %hand_over.1 = (f32[8,2,8,128]{3,2,1,0:T(8,128)}, f32[8,2,8,128]{3,2,1,0:T(8,128)}, f32[8,2,8,128]{3,2,1,0:T(8,128)}) custom-call(f32[8,2,8,128]{3,2,1,0:T(8,128)S(1)} %get-tuple-element.6.sol_in, f32[8,2,8,128]{3,2,1,0:T(8,128)S(1)} %get-tuple-element.7.res_in, f32[8,2,8,128]{3,2,1,0:T(8,128)S(1)} %get-tuple-element.8.dir_in), custom_call_target="tpu_custom_call" | custom-call | tf_op jit(solution)/shard_map/hand_over/pallas_call | solution.py:516
  (1 shorter events, 0.0 us)
Async XLA Ops:
  0.6 1.5 %copy-start = (f32[8,2,8,128]{3,2,1,0:T(8,128)S(1)}, f32[8,2,8,128]{3,2,1,0:T(8,128)}, u32[]{:S(2)}) copy-start(f32[8,2,8,128]{3,2,1,0:T(8,128)} %rhs_ref.1) | copy-start | bytes 196612

commit v7 on v6

--- a/solution.py
+++ b/solution.py
@@ -261,7 +261,7 @@
 
     pending = []
 
-    def correct(source, call):
+    def correct(source, call, meanwhile=lambda: None):
         def z(p):
             return source(p) * weight[p]
 
@@ -278,6 +278,7 @@
             own_c.at[call, pl.ds(0, HALO)], own_c.at[call, pl.ds(group - HALO, HALO)],
             halo_c.at[call, 0], halo_c.at[call, 1], call)
         pending.append(copies)
+        meanwhile()
         finish_edges(*copies)
 
         def swept(cell):
@@ -346,11 +347,6 @@
             u = halo_a[1, (p - hi) // 2, (p - hi) % 2]
         return u.reshape(shape)
 
-    correct(product_plane, 1)
-    for p, u in smoothed(product_plane, lo, hi):
-        keep(2, p, u)
-    send_back(1, 2, 1)
-
     def flat(block):
         parts = []
         for a in range(lx):
@@ -358,10 +354,20 @@
             parts += [turned[b] for b in range(ly)]
         return jnp.concatenate(parts, axis=1)
 
-    given = flat(rhs_ref[...])
-    for j in others:
-        wait_back(0, 0, 2, j)
-    field, product = flat(returned[0]), flat(returned[1])
+    flats = []
+
+    def flatten():
+        flats.append(flat(rhs_ref[...]))
+        for j in others:
+            wait_back(0, 0, 2, j)
+        flats.extend((flat(returned[0]), flat(returned[1])))
+
+    correct(product_plane, 1, flatten)
+    given, field, product = flats
+    for p, u in smoothed(product_plane, lo, hi):
+        keep(2, p, u)
+    send_back(1, 2, 1)
+
     for j in others:
         wait_back(1, 2, 1, j)
     twice = flat(returned[2])

time: 38.6 us -> 38.6 us (level)
  no operation moved by 1% of the time
where the time goes in v7:
time: 38.6 us; the launch traced here: 38.3 us
  Pallas kernels  36.2 us (94%)
  other arithmetic  1.44 us (4%)
  between operations  0.65 us (2%)
    pallas_call x1, Pallas kernels, local(): pl.pallas_call(functools.partial(kernel, ngx, ngy), out_shape=[jax.ShapeD...  35.5 us
    another operation x3, other arithmetic, local(): jnp.stack([0.001 + density * density * density, supports.astype(f32)])  1.44 us

profile of v7, /device:TPU:0, one launch (start us, length us, event | category | flops | bytes accessed | tf_op | source)
XLA Modules:
  0.0 38.3 jit_solution(13376753351270790761)
XLA Ops:
  0.6 0.0 copy-start
  0.6 0.7 %fusion.1 = f32[1,2,8,128]{3,2,1,0:T(8,128)S(1)} fusion(s32[2,8,128]{2,1,0:T(8,128)} %param.4), kind=kLoop, calls=%fused_computation.3 | loop fusion | flops 12288 | bytes 16384 | tf_op jit(solution)/shard_map/stack | solution.py:488
  1.4 0.7 %convert_bitcast_fusion = f32[1,2,8,128]{3,2,1,0:T(8,128)S(1)} fusion(s32[2,8,128]{2,1,0:T(8,128)} %param.5), kind=kLoop, calls=%fused_computation.4 | loop fusion | flops 2048 | bytes 16384 | tf_op jit(solution)/shard_map/stack | solution.py:488
  2.1 0.0 copy-done
  2.1 35.5 %block_step.1 = (f32[8,2,8,128]{3,2,1,0:T(8,128)S(1)}, f32[8,2,8,128]{3,2,1,0:T(8,128)S(1)}, f32[8,2,8,128]{3,2,1,0:T(8,128)S(1)}) custom-call(f32[8,2,8,128]{3,2,1,0:T(8,128)S(1)} %copy-done, f32[2,2,8,128]{3,2,1,0:T(8,128)S(1)} %pad_maximum_fusion.mine), custom_call_target="tpu_custom_call" | custom-call | tf_op jit(solution)/shard_map/block_step/pallas_call | solution.py:489
  37.6 0.7 %hand_over.1 = (f32[8,2,8,128]{3,2,1,0:T(8,128)}, f32[8,2,8,128]{3,2,1,0:T(8,128)}, f32[8,2,8,128]{3,2,1,0:T(8,128)}) custom-call(f32[8,2,8,128]{3,2,1,0:T(8,128)S(1)} %get-tuple-element.6.sol_in, f32[8,2,8,128]{3,2,1,0:T(8,128)S(1)} %get-tuple-element.7.res_in, f32[8,2,8,128]{3,2,1,0:T(8,128)S(1)} %get-tuple-element.8.dir_in), custom_call_target="tpu_custom_call" | custom-call | tf_op jit(solution)/shard_map/hand_over/pallas_call | solution.py:522
  (1 shorter events, 0.0 us)
Async XLA Ops:
  0.6 1.5 %copy-start = (f32[8,2,8,128]{3,2,1,0:T(8,128)S(1)}, f32[8,2,8,128]{3,2,1,0:T(8,128)}, u32[]{:S(2)}) copy-start(f32[8,2,8,128]{3,2,1,0:T(8,128)} %rhs_ref.1) | copy-start | bytes 196612
